TPU v7x, 32 devices: a whole 2x2x4 slice. The times are simulated.
32 devices in a mesh: macro: 8 (over z, y), pool: 4 (over x, core).
Axes of the slice: x: 2, y: 2, z: 4, core: 2. Of those that a mesh axis runs over, the one named last changes fastest.
Arguments:
- history: float32 [729, 16384], P(None, ('macro', 'pool')), may hold values from -6 to 6
- yield_flags: int32 [729, 16384], P(None, ('macro', 'pool')), may hold values 0 or 1
- strain: float32 [6, 16384], P(None, ('macro', 'pool')), may hold values from -6 to 6
- qp_to_rve: int32 [32, 512], P(('macro', 'pool')), may hold values from 0 to 511, each once within a row
- new_owner: int32 [16384, 1], P(('macro', 'pool')), may hold values from 0 to 31; in each aligned block of 512 rows (0 to 511, 512 to 1023, ...) at most 32 rows name the same one
- stiffness: float32 [9, 9, 81, 81], replicated, as said below
- pattern: int32 [9, 9], replicated, may hold values from 0 to 1, as said below
- coupling: float32 [3, 6, 729], replicated, as said below
- plastic_dir: float32 [3, 729], replicated, may hold values from -6 to 6
Outputs:
- new_history: float32 [729, 32768], P(None, ('macro', 'pool'))
- stress: float32 [6, 16384], P(None, ('macro', 'pool'))
Inputs may be any that keep to these rules, and one draw needn't show every extreme that they name: `new_owner`: among the rows of one device no owner is named more than 32 times, a bound that some block reaches. `qp_to_rve`: each row is a permutation of 0 to 511. `pattern`: Symmetric, with ones on the diagonal. stiffness[a, b] is the transpose of stiffness[b, a]; diagonal entries of diagonal blocks lie in 0.5 to 1.5, all others in 0 to 0.032. `coupling`: entries lie in -5.7 to 6.3.
All inputs are finite; a program needn't handle non-finite values. No bound on the sum of `yield_flags` on one device may be relied on, other than what follows from the above.
Results may differ from a plain program's by a relative error of at most 0.0003.
Values sent between devices are 32-bit elements; how exact they have to be, the bound alone decides.
No kernel may reach another device: no remote copies, remote signals or barrier semaphores. Data moves between devices by JAX's collectives and lax.ppermute only.
A program may use at most 128 MiB of HBM per device.

v0:
```python
import functools
import math

import jax
import jax.numpy as jnp
from jax import lax
from jax.experimental import pallas as pl
from jax.experimental.pallas import tpu as pltpu
from jax.sharding import PartitionSpec as P

ITERS = 3
LANES = 128
PLANES = 4

NN = (((1,), (0,)), ((), ()))
NT = (((1,), (1,)), ((), ()))
TN = (((0,), (0,)), ((), ()))


def up(value, unit):
    return -(-value // unit) * unit


def dot(a, b, dims=NN):
    return lax.dot_general(a, b, dims, preferred_element_type=jnp.float32)


def halves(x):
    hi = x.astype(jnp.bfloat16)
    lo = (x - hi.astype(jnp.float32)).astype(jnp.bfloat16)
    return hi, lo


def whereabouts(devices):
    me = lax.axis_index("macro") * lax.axis_size("pool") + lax.axis_index("pool")
    lanes = devices // PLANES
    return me, me // lanes, me % lanes, lanes


def hot(row, count):
    rows = lax.broadcasted_iota(jnp.int32, (count, row.shape[1]), 0)
    return jnp.where(rows == row, 1.0, 0.0).astype(jnp.bfloat16)


def prep_kernel(devices, per_peer, owner, qp, hist, flag, strain, stiff, pattern, coupling, plastic,
                khi, klo, hist_s, weight_s, strain_s, place_s, qp_s, cstack, pdir, kfull, pad):
    nodes, columns = hist.shape
    rows = hist_s.shape[0]
    nb, blk = stiff.shape[0], stiff.shape[2]
    comps, voigt = coupling.shape[0], coupling.shape[1]

    kfull[...] = jnp.zeros_like(kfull)
    for a in range(nb):
        for b in range(nb):
            kfull[a * blk:(a + 1) * blk, b * blk:(b + 1) * blk] = (
                stiff[a, b] * pattern[a, b].astype(jnp.float32)
            )
    k = kfull[...]
    kh = k.astype(jnp.bfloat16)
    khi[...] = kh
    klo[...] = (k - kh.astype(jnp.float32)).astype(jnp.bfloat16)

    me, plane, lane, lanes = whereabouts(devices)
    half = lanes // 2
    apart = owner[...] // lanes ^ plane
    target = owner[...] % lanes
    across = (target ^ lane) % lanes // half
    there = across * half + jnp.where(across == 0, target % half, (target ^ lane) % half)
    turn = jnp.where(apart == 2, 0, jnp.where(apart == 3, 1, jnp.where(apart == 1, 2, 3)))
    key = turn * lanes + jnp.where(apart == 3, there, target)
    key_ids = lax.broadcasted_iota(jnp.int32, (devices, columns), 0)
    mine = jnp.where(key_ids == key, 1.0, 0.0)
    earlier = jnp.where(
        lax.broadcasted_iota(jnp.int32, (columns, columns), 0)
        < lax.broadcasted_iota(jnp.int32, (columns, columns), 1), 1.0, 0.0
    ).astype(jnp.bfloat16)
    before = dot(mine.astype(jnp.bfloat16), earlier)
    rank = jnp.sum(before * mine, axis=0, keepdims=True)
    tally = jnp.sum(mine, axis=1, keepdims=True)
    ahead = jnp.where(key_ids < key, tally, 0.0)
    position = (rank + jnp.sum(ahead, axis=0, keepdims=True)).astype(jnp.int32)

    order = hot(position, columns)
    for source, target in ((hist, hist_s),):
        hi, lo = halves(source[...])
        target[...] = jnp.zeros_like(target)
        target[0:nodes, :] = dot(hi, order, NT) + dot(lo, order, NT)
    h = hist_s[...]
    weight_s[...] = jnp.zeros_like(weight_s)
    weight_s[0:nodes, :] = dot(flag[...].astype(jnp.float32).astype(jnp.bfloat16), order, NT)
    weight_s[...] = weight_s[...] * h * h / (1.0 + h * h)

    pad[...] = jnp.zeros_like(pad)
    pad[0:1, :] = key.astype(jnp.float32)
    pad[1:2, :] = rank
    placed = dot(pad[...].astype(jnp.bfloat16), order, NT)
    place_s[...] = jnp.broadcast_to(
        (placed[0:1, :] * per_peer + placed[1:2, :]).astype(jnp.int32), place_s.shape
    )

    pad[0:1, :] = (position // 256).astype(jnp.float32)
    pad[1:2, :] = (position % 256).astype(jnp.float32)
    found = dot(pad[...].astype(jnp.bfloat16), hot(qp[...], columns))
    at = (found[0:1, :] * 256.0 + found[1:2, :]).astype(jnp.int32)
    qp_s[...] = jnp.broadcast_to(at, qp_s.shape)
    pad[...] = jnp.zeros_like(pad)
    pad[0:voigt, :] = strain[...]
    hi, lo = halves(pad[...])
    serves = hot(at, columns)
    strain_s[...] = dot(hi, serves, NT) + dot(lo, serves, NT)

    cstack[...] = jnp.zeros_like(cstack)
    for c in range(comps):
        cpl = coupling[c]
        hi = cpl.astype(jnp.bfloat16).astype(jnp.float32)
        cstack[c, 0:voigt, 0:nodes] = hi
        cstack[c, 8:8 + voigt, 0:nodes] = hi
        cstack[c, 16:16 + voigt, 0:nodes] = cpl - hi
    pdir[...] = jnp.zeros_like(pdir)
    for c in range(comps):
        spread = jnp.broadcast_to(plastic[c:c + 1, :], (LANES, nodes))
        pdir[c, 0:nodes, :] = jnp.transpose(spread)


def sweep(rows, comps):
    cuts = [rows // 16 * i // 4 * 16 for i in range(5)]
    for top, end in zip(cuts, cuts[1:]):
        for c in range(comps):
            yield slice(top, end), slice(c * LANES, (c + 1) * LANES), c


def fold(x):
    return jnp.sum(x.reshape(x.shape[0] // 8, 8, x.shape[1]), axis=0)


def total(parts):
    return jnp.sum(parts, axis=0, keepdims=True)


def solve_kernel(scale, first, earlier, khi, klo, hist, weight, strain, cstack, pdir, place,
                 *refs):
    earlier_updated, refs = refs[:earlier], refs[earlier:]
    updated, stress, blocks = refs[0], refs[1], refs[2:-5]
    field, resid, image, solved, split = refs[-5:]
    rows = hist.shape[0]
    comps = pdir.shape[0]
    zero = jnp.zeros((8, LANES), jnp.float32)
    s = strain[...]
    s_hi = s.astype(jnp.bfloat16).astype(jnp.float32)
    s3 = jnp.concatenate([s_hi, s - s_hi, s_hi, jnp.zeros_like(s)], axis=0).astype(jnp.bfloat16)
    wide = comps * LANES
    split[rows:, :] = jnp.zeros((split.shape[0] - rows, 2 * wide), jnp.bfloat16)
    for c in range(comps):
        image[:, c * LANES:(c + 1) * LANES] = dot(cstack[c].astype(jnp.bfloat16), s3, TN)
    parts = zero
    for r, l, c in sweep(rows, comps):
        d = image[r, l] - weight[r, :] * hist[r, :] * pdir[c, r, :]
        resid[r, l] = d
        field[r, l] = d
        split[r, l], split[r, wide + c * LANES:wide + (c + 1) * LANES] = halves(d)
        parts = parts + fold(d * d)
    norm = total(parts)
    for step in range(ITERS):
        both = dot(khi[...], split[...])
        image[...] = both[:, 0:wide] + both[:, wide:] + dot(klo[...], split[:, 0:wide])
        parts = zero
        for r, l, c in sweep(rows, comps):
            d = field[r, l]
            q = image[r, l] + (1.5 - weight[r, :]) * d
            image[r, l] = q
            parts = parts + fold(d * q)
        alpha = norm / jnp.maximum(total(parts), 1.0)
        if step == ITERS - 1:
            break
        parts = zero
        for r, l, c in sweep(rows, comps):
            gain = alpha * field[r, l]
            solved[r, l] = gain if step == 0 else solved[r, l] + gain
            left = resid[r, l] - alpha * image[r, l]
            resid[r, l] = left
            parts = parts + fold(left * left)
        following = total(parts)
        beta = following / jnp.maximum(norm, 1.0)
        norm = following
        for r, l, c in sweep(rows, comps):
            d = resid[r, l] + beta * field[r, l]
            field[r, l] = d
            split[r, l], split[r, wide + c * LANES:wide + (c + 1) * LANES] = halves(d)
    for r, l, c in sweep(rows, comps):
        x = solved[r, l] + alpha * field[r, l]
        flow = pdir[c, r, :] * x
        image[r, 0:LANES] = flow if c == 0 else image[r, 0:LANES] + flow
        split[r, l], split[r, wide + c * LANES:wide + (c + 1) * LANES] = halves((1.5 - weight[r, :]) * x)
    updated[...] = hist[...] + weight[...] * image[:, 0:LANES]
    place_blocks(first, place, [*earlier_updated, updated], blocks)
    out = s
    for c in range(comps):
        l = slice(c * LANES, (c + 1) * LANES)
        cpl = cstack[c].astype(jnp.bfloat16)
        main = dot(cpl, split[0:rows, l])
        minor = dot(cpl, split[0:rows, wide + c * LANES:wide + (c + 1) * LANES])
        out = out + scale * (main[0:8] + main[16:24] + minor[0:8])
    stress[...] = out


def place_blocks(first, place, sources, blocks):
    rows = sources[0].shape[0]
    count = sum(block.shape[0] for block in blocks)
    width = LANES * len(sources)
    placing = hot(place[0:1, 0:width] - first, count)
    sums = 0.0
    for i, source in enumerate(sources):
        hi, lo = halves(source[...])
        cut = placing[:, i * LANES:(i + 1) * LANES]
        sums = sums + (dot(cut, hi, NT) + dot(cut, lo, NT))
    top = 0
    for block in blocks:
        block[:, 0:rows] = sums[top:top + block.shape[0], :]
        block[:, rows:] = jnp.zeros((block.shape[0], block.shape[1] - rows), jnp.float32)
        top += block.shape[0]


def ship_kernel(first, chunks, place, *refs):
    place_blocks(first, place, refs[:chunks], refs[chunks:])


def land_kernel(devices, cap, two, near, one, own, *refs):
    direct, out, stage = refs[:-2], refs[-2], refs[-1]
    nodes = out.shape[0]
    me, plane, lane, lanes = whereabouts(devices)
    half = lanes // 2
    span = half * cap

    def land(tile, at):
        columns = pl.multiple_of(at * span, LANES)
        out[:, pl.ds(columns, span)] = jnp.transpose(tile)[0:nodes, :]

    for arrived, apart in ((own, 0), (two, 2), (one, 1)):
        for part in range(2):
            land(arrived[part * span:(part + 1) * span, :], (plane ^ apart) * 2 + part)
    side = lane // half
    land(near[...], (plane ^ 3) * 2 + side)
    for i, block in enumerate(direct):
        at = pl.multiple_of(((lane % half) ^ i) * cap, cap)
        stage[pl.ds(at, cap), :] = block[...]
    columns = pl.multiple_of(((plane ^ 3) * 2 + 1 - side) * span, LANES)
    out[:, pl.ds(columns, span)] = jnp.transpose(stage[...])[0:nodes, :]


def back_kernel(at, *refs):
    out = refs[-1]
    stress = jnp.concatenate([ref[...] for ref in refs[:-1]], axis=1)
    serves = hot(at[0:1, :], stress.shape[1])
    hi, lo = halves(stress)
    out[...] = (dot(hi, serves) + dot(lo, serves))[0:out.shape[0], :]


def params():
    return pltpu.CompilerParams(vmem_limit_bytes=56 * 2**20)


def shards(
    history, yield_flags, strain, qp_to_rve, new_owner, stiffness, pattern, coupling, plastic_dir
):
    devices = lax.axis_size(("macro", "pool"))
    nodes, columns = history.shape
    comps, voigt = coupling.shape[0], coupling.shape[1]
    per_peer = 2 * columns // devices
    rows = up(nodes, 32)
    deep = up(nodes, 256)
    f32, bf16, i32 = jnp.float32, jnp.bfloat16, jnp.int32
    vmem = pl.BlockSpec(memory_space=pltpu.VMEM)
    smem = pl.BlockSpec(memory_space=pltpu.SMEM)
    khi, klo, hist_s, weight_s, strain_s, place_s, qp_s, cstack, pdir = pl.pallas_call(
        functools.partial(prep_kernel, devices, per_peer),
        out_shape=(
            jax.ShapeDtypeStruct((rows, deep), bf16),
            jax.ShapeDtypeStruct((rows, deep), bf16),
            jax.ShapeDtypeStruct((rows, columns), f32),
            jax.ShapeDtypeStruct((rows, columns), f32),
            jax.ShapeDtypeStruct((8, columns), f32),
            jax.ShapeDtypeStruct((8, columns), i32),
            jax.ShapeDtypeStruct((8, columns), i32),
            jax.ShapeDtypeStruct((comps, 32, rows), f32),
            jax.ShapeDtypeStruct((comps, rows, LANES), f32),
        ),
        in_specs=[vmem] * 6 + [smem] + [vmem] * 2,
        out_specs=[vmem] * 9,
        scratch_shapes=[pltpu.VMEM((rows, deep), f32), pltpu.VMEM((8, columns), f32)],
        compiler_params=params(),
    )(new_owner.reshape(1, columns), qp_to_rve, history, yield_flags, strain, stiffness, pattern,
      coupling, plastic_dir)

    chunks = columns // LANES
    lanes = devices // PLANES
    half = lanes // 2
    wide = comps * LANES
    block = lambda height: jax.ShapeDtypeStruct((height, deep), f32)
    whole = lambda shape: pl.BlockSpec(shape, lambda i: (0,) * len(shape))
    updated, stress_s, ready = [], [], []
    for k in range(chunks):
        part = lambda height: pl.BlockSpec((height, LANES), lambda i, k=k: (0, k))
        outs = [block(half * per_peer)] if k < 3 else [block(per_peer)] * half
        done = pl.pallas_call(
            functools.partial(solve_kernel, 1.0 / math.sqrt(comps * nodes), k * LANES, k),
            grid=(1,),
            out_shape=(
                jax.ShapeDtypeStruct((rows, LANES), f32),
                jax.ShapeDtypeStruct((8, LANES), f32),
                *outs,
            ),
            in_specs=[whole((rows, deep)), whole((rows, deep)), part(rows), part(rows), part(8),
                      whole((comps, 32, rows)), whole((comps, rows, LANES)), whole((8, columns))]
            + [whole((rows, LANES))] * k,
            out_specs=[whole((rows, LANES)), whole((8, LANES))] + [whole(o.shape) for o in outs],
            scratch_shapes=[pltpu.VMEM((rows, wide), f32) for _ in range(4)]
            + [pltpu.VMEM((deep, 2 * wide), bf16)],
            compiler_params=params(),
            cost_estimate=pl.CostEstimate(
                flops=18 * rows * deep * wide, bytes_accessed=8 * 2**20, transcendentals=0
            ),
        )(khi, klo, hist_s, weight_s, strain_s, cstack, pdir, place_s, *updated)
        updated.append(done[0])
        stress_s.append(done[1])
        ready.append(done[2:])
    last = pl.pallas_call(
        functools.partial(ship_kernel, chunks * LANES, chunks),
        out_shape=(block(lanes * per_peer),) * 2,
        in_specs=[vmem] * (1 + chunks),
        out_specs=[vmem] * 2,
        compiler_params=params(),
        cost_estimate=pl.CostEstimate(
            flops=4 * rows * columns * columns, bytes_accessed=4 * 2**20, transcendentals=0
        ),
    )(place_s, *updated)

    axes = ("macro", "pool")

    def hop(sent, mask):
        return lax.ppermute(sent, axes, [(s, s ^ mask) for s in range(devices)])

    def spread(sent, size):
        groups = [list(range(first, first + size)) for first in range(0, devices, size)]
        shape = sent.shape
        return lax.all_to_all(
            sent.reshape(size, per_peer, deep), axes, split_axis=0, concat_axis=0,
            axis_index_groups=groups, tiled=True,
        ).reshape(shape)

    two_a, two_b = hop(ready[0][0], 2 * lanes), hop(ready[1][0], 2 * lanes)
    near = hop(ready[2][0], 3 * lanes)
    direct = [hop(sent, 3 * lanes + half + i) for i, sent in enumerate(ready[3])]
    one = hop(last[0], lanes)
    two_a, two_b, own = lax.optimization_barrier((two_a, two_b, last[1]))
    own = spread(own, lanes)
    two = spread(jnp.concatenate([two_a, two_b], axis=0), lanes)
    near, two, own = lax.optimization_barrier((near, two, own))
    near = spread(near, half)
    one = spread(one, lanes)
    new_history = pl.pallas_call(
        functools.partial(land_kernel, devices, per_peer),
        out_shape=jax.ShapeDtypeStruct((nodes, devices * per_peer), f32),
        in_specs=[vmem] * (4 + half),
        out_specs=vmem,
        scratch_shapes=[pltpu.VMEM((LANES, deep), f32)],
        compiler_params=params(),
    )(two, near, one, own, *direct)
    stress_out = pl.pallas_call(
        back_kernel,
        out_shape=jax.ShapeDtypeStruct((voigt, columns), f32),
        in_specs=[vmem] * (1 + chunks),
        out_specs=vmem,
        compiler_params=params(),
    )(qp_s, *stress_s)
    return (new_history, stress_out)


def solution(mesh):
    return jax.shard_map(
        shards,
        mesh=mesh,
        in_specs=(
            P(None, ("macro", "pool")),
            P(None, ("macro", "pool")),
            P(None, ("macro", "pool")),
            P(("macro", "pool"), None),
            P(("macro", "pool"), None),
            P(),
            P(),
            P(),
            P(),
        ),
        out_specs=(P(None, ("macro", "pool")), P(None, ("macro", "pool"))),
        check_vma=False,
    )
```

profile of v0, /device:TPU:0, one launch (start us, length us, event | category | flops | bytes accessed | tf_op | source)
XLA Modules:
  0.0 153.8 jit_solution(12580545124705771880)
XLA Ops:
  0.6 8.3 %shard_map.104 = (bf16[736,768]{1,0:T(8,128)(2,1)}, bf16[736,768]{1,0:T(8,128)(2,1)}, f32[736,512]{1,0:T(8,128)}, f32[736,512]{1,0:T(8,128)}, f32[8,512]{1,0:T(8...) custom-call(s32[1,512]{1,0:T(1,128)} %bitcast.14, s32[1,512]{1,0:T(1,128)} %qp.1, ...), custom_call_target="tpu_custom_call" | custom-call | tf_op jit(solution)/shard_map/pallas_call | solution.py:274
  8.9 11.2 %shard_map.105 = (f32[736,128]{1,0:T(8,128)}, f32[8,128]{1,0:T(8,128)}, f32[128,768]{1,0:T(8,128)}) custom-call(bf16[736,768]{1,0:T(8,128)(2,1)} %get-tuple-element.34.khi, bf16[736,768]{1,0:T(8,128)(2,1)} %get-tuple-element.35.klo, f32[736,512]{1,0:T(8,128)} %get-tuple-element.36.hist, f32[736,512]{1,0:T(8,128)} %get-tuple-element.37.weight, ...), custom_call_target="tpu_custom_call" | custom-call | flops 3906994176 | bytes 8388608 | tf_op jit(solution)/shard_map/pallas_call | solution.py:304
  20.1 4.0 %collective-permute-start.1 = (f32[128,768]{1,0:T(8,128)}, f32[128,768]{1,0:T(8,128)S(1)}, u32[]{:S(2)}, u32[]{:S(2)}) collective-permute-start(f32[128,768]{1,0:T(8,128)} %get-tuple-element.45), channel_id=1, source_target_pairs={{0,16},{1,17},{2,18},{3,19},{4,20},{5,21},{6,22},{7,23},{8,24},{9,... | collective-permute-start | bytes 1179656 | tf_op jit(solution)/shard_map/ppermute | solution.py:340
  24.1 11.3 %shard_map.106 = (f32[736,128]{1,0:T(8,128)}, f32[8,128]{1,0:T(8,128)}, f32[128,768]{1,0:T(8,128)}) custom-call(bf16[736,768]{1,0:T(8,128)(2,1)} %get-tuple-element.34.khi, bf16[736,768]{1,0:T(8,128)(2,1)} %get-tuple-element.35.klo, f32[736,512]{1,0:T(8,128)} %get-tuple-element.36.hist, f32[736,512]{1,0:T(8,128)} %get-tuple-element.37.weight, ...), custom_call_target="tpu_custom_call" | custom-call | flops 3906994176 | bytes 8388608 | tf_op jit(solution)/shard_map/pallas_call | solution.py:304
  35.4 11.7 %shard_map.107 = (f32[736,128]{1,0:T(8,128)}, f32[8,128]{1,0:T(8,128)}, f32[128,768]{1,0:T(8,128)}) custom-call(bf16[736,768]{1,0:T(8,128)(2,1)} %get-tuple-element.34.khi, bf16[736,768]{1,0:T(8,128)(2,1)} %get-tuple-element.35.klo, f32[736,512]{1,0:T(8,128)} %get-tuple-element.36.hist, f32[736,512]{1,0:T(8,128)} %get-tuple-element.37.weight, ...), custom_call_target="tpu_custom_call" | custom-call | flops 3906994176 | bytes 8388608 | tf_op jit(solution)/shard_map/pallas_call | solution.py:304
  47.1 12.0 %shard_map.108 = (f32[736,128]{1,0:T(8,128)}, f32[8,128]{1,0:T(8,128)}, f32[32,768]{1,0:T(8,128)}, f32[32,768]{1,0:T(8,128)}, f32[32,768]{1,0:T(8,128)}, /*index=5*/f32[32,768]{1,0:T(8,128)}) custom-call(bf16[736,768]{1,0:T(8,128)(2,1)} %get-tuple-element.34.khi, bf16[736,768]{1,0:T(8,128)(2,1)} %get-tuple-element.35.klo, ...), custom_call_target="tpu_custom_call" | custom-call | flops 3906994176 | bytes 8388608 | tf_op jit(solution)/shard_map/pallas_call | solution.py:304
  59.1 4.3 %shard_map.109 = (f32[256,768]{1,0:T(8,128)}, f32[256,768]{1,0:T(8,128)}) custom-call(s32[8,512]{1,0:T(8,128)} %get-tuple-element.41.place, f32[736,128]{1,0:T(8,128)} %get-tuple-element.42.refs_0_, f32[736,128]{1,0:T(8,128)} %get-tuple-element.43.refs_1_, f32[736,128]{1,0:T(8,128)} %get-tuple-element.47.refs_2_, f32[736,128]{1,0:T(8,128)} %get-tuple-element.48.refs_3_), custom_call_target="tpu_custom_call" | custom-call | flops 771751936 | bytes 4194304 | tf_op jit(solution)/shard_map/pallas_call | solution.py:326
  63.5 16.6 %all_to_all.20 = f32[8,32,768]{2,1,0:T(8,128)} all-to-all(f32[8,32,768]{2,1,0:T(8,128)S(1)} %bitcast.12), channel_id=1, replica_groups={{0,1,2,3,4,5,6,7},{8,9,10,11,12,13,14,15},{16,17,18,19,20,21,22,23},{24..., dimensions={0} | all-to-all | bytes 1572864 | tf_op jit(solution)/shard_map/all_to_all | solution.py:345
  80.1 3.5 %all-to-all-start.1 = ((f32[8,32,768]{2,1,0:T(8,128)}), f32[8,32,768]{2,1,0:T(8,128)S(1)}, u32[]{:S(2)}, u32[]{:S(2)}) async-start(f32[8,32,768]{2,1,0:T(8,128)} %bitcast.3), calls=%async_computation.1 | async-start | bytes 1572864 | tf_op jit(solution)/shard_map/all_to_all | solution.py:345
  83.7 1.7 %collective-permute-start.3 = (f32[256,768]{1,0:T(8,128)S(1)}, f32[256,768]{1,0:T(8,128)}, u32[]{:S(2)}, u32[]{:S(2)}) collective-permute-start(f32[256,768]{1,0:T(8,128)S(1)} %copy-done.7), channel_id=1, source_target_pairs={{0,8},{1,9},{2,10},{3,11},{4,12},{5,13},{6,14},{7,15},{8,0},{9,1},... | collective-permute-start | bytes 2359304 | tf_op jit(solution)/shard_map/ppermute | solution.py:340
  85.4 2.5 %collective-permute-start = (f32[128,768]{1,0:T(8,128)S(1)}, f32[128,768]{1,0:T(8,128)}, u32[]{:S(2)}, u32[]{:S(2)}) collective-permute-start(f32[128,768]{1,0:T(8,128)S(1)} %copy-done.8), channel_id=1, source_target_pairs={{0,24},{1,25},{2,26},{3,27},{4,28},{5,29},{6,30},{7,31},{8,16},{9,... | collective-permute-start | bytes 1179656 | tf_op jit(solution)/shard_map/ppermute | solution.py:340
  87.8 26.3 %collective-permute-done = f32[128,768]{1,0:T(8,128)} collective-permute-done((f32[128,768]{1,0:T(8,128)S(1)}, f32[128,768]{1,0:T(8,128)}, u32[]{:S(2)}, u32[]{:S(2)}) %collective-permute-start) | collective-permute-done | bytes 393248 | tf_op jit(solution)/shard_map/ppermute | solution.py:340
  114.1 3.5 %all-to-all-start.2 = ((f32[4,32,768]{2,1,0:T(8,128)}), f32[4,32,768]{2,1,0:T(8,128)S(1)}, u32[]{:S(2)}, u32[]{:S(2)}) async-start(f32[4,32,768]{2,1,0:T(8,128)} %bitcast.5), calls=%async_computation.2 | async-start | bytes 786432 | tf_op jit(solution)/shard_map/all_to_all | solution.py:345
  117.6 7.4 %all-to-all-done.2 = f32[4,32,768]{2,1,0:T(8,128)S(1)} async-done(((f32[4,32,768]{2,1,0:T(8,128)}), f32[4,32,768]{2,1,0:T(8,128)S(1)}, u32[]{:S(2)}, u32[]{:S(2)}) %all-to-all-start.2) | async-done | bytes 393248 | tf_op jit(solution)/shard_map/all_to_all | solution.py:345
  125.0 3.5 %all-to-all-start.3 = ((f32[8,32,768]{2,1,0:T(8,128)}), f32[8,32,768]{2,1,0:T(8,128)S(1)}, u32[]{:S(2)}, u32[]{:S(2)}) async-start(f32[8,32,768]{2,1,0:T(8,128)} %bitcast.7), calls=%async_computation.3 | async-start | bytes 1572864 | tf_op jit(solution)/shard_map/all_to_all | solution.py:345
  128.6 2.8 %collective-permute-start.4 = (f32[32,768]{1,0:T(8,128)S(1)}, f32[32,768]{1,0:T(8,128)S(1)}, u32[]{:S(2)}, u32[]{:S(2)}) collective-permute-start(f32[32,768]{1,0:T(8,128)S(1)} %copy-done.12), channel_id=1, source_target_pairs={{0,28},{1,29},{2,30},{3,31},{4,24},{5,25},{6,26},{7,27},{8,20},{9,... | collective-permute-start | bytes 294920 | tf_op jit(solution)/shard_map/ppermute | solution.py:340
  131.4 1.6 %collective-permute-start.5 = (f32[32,768]{1,0:T(8,128)S(1)}, f32[32,768]{1,0:T(8,128)S(1)}, u32[]{:S(2)}, u32[]{:S(2)}) collective-permute-start(f32[32,768]{1,0:T(8,128)S(1)} %copy-done.11), channel_id=1, source_target_pairs={{0,29},{1,28},{2,31},{3,30},{4,25},{5,24},{6,27},{7,26},{8,21},{9,... | collective-permute-start | bytes 294920 | tf_op jit(solution)/shard_map/ppermute | solution.py:340
  133.0 3.5 %collective-permute-start.6 = (f32[32,768]{1,0:T(8,128)S(1)}, f32[32,768]{1,0:T(8,128)S(1)}, u32[]{:S(2)}, u32[]{:S(2)}) collective-permute-start(f32[32,768]{1,0:T(8,128)S(1)} %copy-done.10), channel_id=1, source_target_pairs={{0,30},{1,31},{2,28},{3,29},{4,26},{5,27},{6,24},{7,25},{8,22},{9,... | collective-permute-start | bytes 294920 | tf_op jit(solution)/shard_map/ppermute | solution.py:340
  136.5 1.9 %collective-permute-start.7 = (f32[32,768]{1,0:T(8,128)S(1)}, f32[32,768]{1,0:T(8,128)S(1)}, u32[]{:S(2)}, u32[]{:S(2)}) collective-permute-start(f32[32,768]{1,0:T(8,128)S(1)} %copy-done.9), channel_id=1, source_target_pairs={{0,31},{1,30},{2,29},{3,28},{4,27},{5,26},{6,25},{7,24},{8,23},{9,... | collective-permute-start | bytes 294920 | tf_op jit(solution)/shard_map/ppermute | solution.py:340
  138.4 1.6 %shard_map.111 = f32[6,512]{1,0:T(8,128)} custom-call(s32[8,512]{1,0:T(8,128)} %get-tuple-element.61.at, f32[8,128]{1,0:T(8,128)} %get-tuple-element.62.refs_0_, f32[8,128]{1,0:T(8,128)} %get-tuple-element.63.refs_1_, f32[8,128]{1,0:T(8,128)} %get-tuple-element.64.refs_2_, f32[8,128]{1,0:T(8,128)} %get-tuple-element.65.refs_3_), custom_call_target="tpu_custom_call" | custom-call | tf_op jit(solution)/shard_map/pallas_call | solution.py:368
  141.0 3.1 %collective-permute-done.6.refs_2_ = f32[32,768]{1,0:T(8,128)S(1)} collective-permute-done((f32[32,768]{1,0:T(8,128)S(1)}, f32[32,768]{1,0:T(8,128)S(1)}, u32[]{:S(2)}, u32[]{:S(2)}) %collective-permute-start.6) | collective-permute-done | bytes 98336 | tf_op jit(solution)/shard_map/ppermute | solution.py:340
  144.2 1.6 %collective-permute-done.7.refs_3_ = f32[32,768]{1,0:T(8,128)S(1)} collective-permute-done((f32[32,768]{1,0:T(8,128)S(1)}, f32[32,768]{1,0:T(8,128)S(1)}, u32[]{:S(2)}, u32[]{:S(2)}) %collective-permute-start.7) | collective-permute-done | bytes 98336 | tf_op jit(solution)/shard_map/ppermute | solution.py:340
  145.8 2.8 %all-to-all-done.3 = f32[8,32,768]{2,1,0:T(8,128)S(1)} async-done(((f32[8,32,768]{2,1,0:T(8,128)}), f32[8,32,768]{2,1,0:T(8,128)S(1)}, u32[]{:S(2)}, u32[]{:S(2)}) %all-to-all-start.3) | async-done | bytes 786464 | tf_op jit(solution)/shard_map/all_to_all | solution.py:345
  149.5 4.3 %shard_map.110 = f32[729,1024]{1,0:T(8,128)} custom-call(f32[256,768]{1,0:T(8,128)} %bitcast.9, f32[128,768]{1,0:T(8,128)} %bitcast.13, f32[256,768]{1,0:T(8,128)} %bitcast.11, f32[256,768]{1,0:T(8,128)} %bitcast.10, f32[32,768]{1,0:T(8,128)} %copy-done.3, f32[32,768]{1,0:T(8,128)} %copy-done.4, f32[32,768]{1,0:T(8,128)} %copy-done.5, f32[32,768]{1,0:T(8,128)} %copy-done.6), custom_call_target="tpu_custom_call" | custom-call | tf_op jit(solution)/shard_map/pallas_call | solution.py:360
  (34 shorter events, 2.0 us)
Async XLA Ops:
  20.1 43.3 %collective-permute-start.1 = (f32[128,768]{1,0:T(8,128)}, f32[128,768]{1,0:T(8,128)S(1)}, u32[]{:S(2)}, u32[]{:S(2)}) collective-permute-start(f32[128,768]{1,0:T(8,128)} %get-tuple-element.45), channel_id=1, source_target_pairs={{0,16},{1,17},{2,18},{3,19},{4,20},{5,21},{6,22},{7,23},{8,24},{9,... | collective-permute-start | bytes 1179656 | tf_op jit(solution)/shard_map/ppermute | solution.py:340
  35.4 28.0 %collective-permute-start.2 = (f32[128,768]{1,0:T(8,128)}, f32[128,768]{1,0:T(8,128)S(1)}, u32[]{:S(2)}, u32[]{:S(2)}) collective-permute-start(f32[128,768]{1,0:T(8,128)} %get-tuple-element.46), channel_id=1, source_target_pairs={{0,16},{1,17},{2,18},{3,19},{4,20},{5,21},{6,22},{7,23},{8,24},{9,... | collective-permute-start | bytes 1179656 | tf_op jit(solution)/shard_map/ppermute | solution.py:340
  63.4 20.3 %copy-start.7 = (f32[256,768]{1,0:T(8,128)S(1)}, f32[256,768]{1,0:T(8,128)}, u32[]{:S(2)}) copy-start(f32[256,768]{1,0:T(8,128)} %get-tuple-element.55) | copy-start | bytes 2359300
  63.4 21.9 %copy-start.8 = (f32[128,768]{1,0:T(8,128)S(1)}, f32[128,768]{1,0:T(8,128)}, u32[]{:S(2)}) copy-start(f32[128,768]{1,0:T(8,128)} %get-tuple-element.44) | copy-start | bytes 1179652
  80.1 34.1 %all-to-all-start.1 = ((f32[8,32,768]{2,1,0:T(8,128)}), f32[8,32,768]{2,1,0:T(8,128)S(1)}, u32[]{:S(2)}, u32[]{:S(2)}) async-start(f32[8,32,768]{2,1,0:T(8,128)} %bitcast.3), calls=%async_computation.1 | async-start | bytes 1572864 | tf_op jit(solution)/shard_map/all_to_all | solution.py:345
  83.6 44.9 %copy-start.12 = (f32[32,768]{1,0:T(8,128)S(1)}, f32[32,768]{1,0:T(8,128)}, u32[]{:S(2)}) copy-start(f32[32,768]{1,0:T(8,128)} %get-tuple-element.57) | copy-start | bytes 294916
  83.7 47.8 %copy-start.11 = (f32[32,768]{1,0:T(8,128)S(1)}, f32[32,768]{1,0:T(8,128)}, u32[]{:S(2)}) copy-start(f32[32,768]{1,0:T(8,128)} %get-tuple-element.58) | copy-start | bytes 294916
  83.7 49.4 %copy-start.10 = (f32[32,768]{1,0:T(8,128)S(1)}, f32[32,768]{1,0:T(8,128)}, u32[]{:S(2)}) copy-start(f32[32,768]{1,0:T(8,128)} %get-tuple-element.59) | copy-start | bytes 294916
  83.7 52.9 %copy-start.9 = (f32[32,768]{1,0:T(8,128)S(1)}, f32[32,768]{1,0:T(8,128)}, u32[]{:S(2)}) copy-start(f32[32,768]{1,0:T(8,128)} %get-tuple-element.60) | copy-start | bytes 294916
  83.7 33.9 %collective-permute-start.3 = (f32[256,768]{1,0:T(8,128)S(1)}, f32[256,768]{1,0:T(8,128)}, u32[]{:S(2)}, u32[]{:S(2)}) collective-permute-start(f32[256,768]{1,0:T(8,128)S(1)} %copy-done.7), channel_id=1, source_target_pairs={{0,8},{1,9},{2,10},{3,11},{4,12},{5,13},{6,14},{7,15},{8,0},{9,1},... | collective-permute-start | bytes 2359304 | tf_op jit(solution)/shard_map/ppermute | solution.py:340
  85.4 28.8 %collective-permute-start = (f32[128,768]{1,0:T(8,128)S(1)}, f32[128,768]{1,0:T(8,128)}, u32[]{:S(2)}, u32[]{:S(2)}) collective-permute-start(f32[128,768]{1,0:T(8,128)S(1)} %copy-done.8), channel_id=1, source_target_pairs={{0,24},{1,25},{2,26},{3,27},{4,28},{5,29},{6,30},{7,31},{8,16},{9,... | collective-permute-start | bytes 1179656 | tf_op jit(solution)/shard_map/ppermute | solution.py:340
  114.1 34.4 %copy-start = (f32[8,32,768]{2,1,0:T(8,128)}, f32[8,32,768]{2,1,0:T(8,128)S(1)}, u32[]{:S(2)}) copy-start(f32[8,32,768]{2,1,0:T(8,128)S(1)} %all-to-all-done.1) | copy-start | bytes 2359300
  114.1 10.9 %all-to-all-start.2 = ((f32[4,32,768]{2,1,0:T(8,128)}), f32[4,32,768]{2,1,0:T(8,128)S(1)}, u32[]{:S(2)}, u32[]{:S(2)}) async-start(f32[4,32,768]{2,1,0:T(8,128)} %bitcast.5), calls=%async_computation.2 | async-start | bytes 786432 | tf_op jit(solution)/shard_map/all_to_all | solution.py:345
  125.0 23.6 %copy-start.2 = (f32[4,32,768]{2,1,0:T(8,128)}, f32[4,32,768]{2,1,0:T(8,128)S(1)}, u32[]{:S(2)}) copy-start(f32[4,32,768]{2,1,0:T(8,128)S(1)} %all-to-all-done.2) | copy-start | bytes 1179652
  125.0 23.6 %all-to-all-start.3 = ((f32[8,32,768]{2,1,0:T(8,128)}), f32[8,32,768]{2,1,0:T(8,128)S(1)}, u32[]{:S(2)}, u32[]{:S(2)}) async-start(f32[8,32,768]{2,1,0:T(8,128)} %bitcast.7), calls=%async_computation.3 | async-start | bytes 1572864 | tf_op jit(solution)/shard_map/all_to_all | solution.py:345
  128.6 11.5 %collective-permute-start.4 = (f32[32,768]{1,0:T(8,128)S(1)}, f32[32,768]{1,0:T(8,128)S(1)}, u32[]{:S(2)}, u32[]{:S(2)}) collective-permute-start(f32[32,768]{1,0:T(8,128)S(1)} %copy-done.12), channel_id=1, source_target_pairs={{0,28},{1,29},{2,30},{3,31},{4,24},{5,25},{6,26},{7,27},{8,20},{9,... | collective-permute-start | bytes 294920 | tf_op jit(solution)/shard_map/ppermute | solution.py:340
  131.4 9.6 %collective-permute-start.5 = (f32[32,768]{1,0:T(8,128)S(1)}, f32[32,768]{1,0:T(8,128)S(1)}, u32[]{:S(2)}, u32[]{:S(2)}) collective-permute-start(f32[32,768]{1,0:T(8,128)S(1)} %copy-done.11), channel_id=1, source_target_pairs={{0,29},{1,28},{2,31},{3,30},{4,25},{5,24},{6,27},{7,26},{8,21},{9,... | collective-permute-start | bytes 294920 | tf_op jit(solution)/shard_map/ppermute | solution.py:340
  133.0 11.1 %collective-permute-start.6 = (f32[32,768]{1,0:T(8,128)S(1)}, f32[32,768]{1,0:T(8,128)S(1)}, u32[]{:S(2)}, u32[]{:S(2)}) collective-permute-start(f32[32,768]{1,0:T(8,128)S(1)} %copy-done.10), channel_id=1, source_target_pairs={{0,30},{1,31},{2,28},{3,29},{4,26},{5,27},{6,24},{7,25},{8,22},{9,... | collective-permute-start | bytes 294920 | tf_op jit(solution)/shard_map/ppermute | solution.py:340
  136.5 9.3 %collective-permute-start.7 = (f32[32,768]{1,0:T(8,128)S(1)}, f32[32,768]{1,0:T(8,128)S(1)}, u32[]{:S(2)}, u32[]{:S(2)}) collective-permute-start(f32[32,768]{1,0:T(8,128)S(1)} %copy-done.9), channel_id=1, source_target_pairs={{0,31},{1,30},{2,29},{3,28},{4,27},{5,26},{6,25},{7,24},{8,23},{9,... | collective-permute-start | bytes 294920 | tf_op jit(solution)/shard_map/ppermute | solution.py:340
  140.1 8.5 %copy-start.3 = (f32[32,768]{1,0:T(8,128)}, f32[32,768]{1,0:T(8,128)S(1)}, u32[]{:S(2)}) copy-start(f32[32,768]{1,0:T(8,128)S(1)} %collective-permute-done.4.refs_0_) | copy-start | bytes 294916
  141.0 7.5 %copy-start.4 = (f32[32,768]{1,0:T(8,128)}, f32[32,768]{1,0:T(8,128)S(1)}, u32[]{:S(2)}) copy-start(f32[32,768]{1,0:T(8,128)S(1)} %collective-permute-done.5.refs_1_) | copy-start | bytes 294916
  144.2 4.4 %copy-start.5 = (f32[32,768]{1,0:T(8,128)}, f32[32,768]{1,0:T(8,128)S(1)}, u32[]{:S(2)}) copy-start(f32[32,768]{1,0:T(8,128)S(1)} %collective-permute-done.6.refs_2_) | copy-start | bytes 294916
  145.8 2.8 %copy-start.6 = (f32[32,768]{1,0:T(8,128)}, f32[32,768]{1,0:T(8,128)S(1)}, u32[]{:S(2)}) copy-start(f32[32,768]{1,0:T(8,128)S(1)} %collective-permute-done.7.refs_3_) | copy-start | bytes 294916
  148.6 0.9 copy-start.1
where the time goes:
time: 154 us
  Pallas kernels  64.6 us (42%)
  waiting for transfers between devices  42.2 us (27%)
  starting transfers between devices  28.6 us (19%)
  blocking collectives  16.6 us (11%)
    pallas_call x4, Pallas kernels, shards(): pl.pallas_call(functools.partial(solve_kernel, 1.0 / math.sqrt(comps * no...  46.1 us
    ppermute x8, waiting for transfers between devices, hop(): return lax.ppermute(sent, axes, [(s, s ^ mask) for s in range(devices)])  32 us
    ppermute x8, starting transfers between devices, hop(): return lax.ppermute(sent, axes, [(s, s ^ mask) for s in range(devices)])  18 us
    all_to_all x1, blocking collectives, spread(): lax.all_to_all(sent.reshape(size, per_peer, deep), axes, split_axis=0, co...  16.6 us
    all_to_all x3, starting transfers between devices, spread(): lax.all_to_all(sent.reshape(size, per_peer, deep), axes, split_axis=0, co...  10.6 us
    all_to_all x3, waiting for transfers between devices, spread(): lax.all_to_all(sent.reshape(size, per_peer, deep), axes, split_axis=0, co...  10.2 us
    pallas_call x1, Pallas kernels, shards(): pl.pallas_call(functools.partial(prep_kernel, devices, per_peer), out_sha...  8.28 us
    pallas_call x1, Pallas kernels, shards(): pl.pallas_call(functools.partial(land_kernel, devices, per_peer), out_sha...  4.31 us
  transfers between devices with their start and end apart: 11, of which 6 were waited for; matrix products, arithmetic and copies ran while one was open for 0% of the time, Pallas kernels for 27%

commit v1 on v0

--- a/solution.py
+++ b/solution.py
@@ -65,8 +65,8 @@
     apart = owner[...] // lanes ^ plane
     target = owner[...] % lanes
     across = (target ^ lane) % lanes // half
-    there = across * half + jnp.where(across == 0, target % half, (target ^ lane) % half)
-    turn = jnp.where(apart == 2, 0, jnp.where(apart == 3, 1, jnp.where(apart == 1, 2, 3)))
+    there = across * half + target % half
+    turn = jnp.where(apart == 2, 0, jnp.where(apart == 1, 1, jnp.where(apart == 3, 2, 3)))
     key = turn * lanes + jnp.where(apart == 3, there, target)
     key_ids = lax.broadcasted_iota(jnp.int32, (devices, columns), 0)
     mine = jnp.where(key_ids == key, 1.0, 0.0)
@@ -224,27 +224,34 @@
     place_blocks(first, place, refs[:chunks], refs[chunks:])
 
 
-def land_kernel(devices, cap, two, near, one, own, *refs):
-    direct, out, stage = refs[:-2], refs[-2], refs[-1]
+def land(tile, out, stage, sem, slot, at):
     nodes = out.shape[0]
+    stage[slot] = jnp.transpose(tile)[0:nodes, :]
+    columns = pl.multiple_of(at * LANES, LANES)
+    copy = pltpu.make_async_copy(stage.at[slot], out.at[:, pl.ds(columns, LANES)], sem.at[slot])
+    copy.start()
+    return copy
+
+
+def land_kernel(devices, two, one, own, out, stage, sem):
     me, plane, lane, lanes = whereabouts(devices)
-    half = lanes // 2
-    span = half * cap
-
-    def land(tile, at):
-        columns = pl.multiple_of(at * span, LANES)
-        out[:, pl.ds(columns, span)] = jnp.transpose(tile)[0:nodes, :]
-
+    copies = []
     for arrived, apart in ((own, 0), (two, 2), (one, 1)):
-        for part in range(2):
-            land(arrived[part * span:(part + 1) * span, :], (plane ^ apart) * 2 + part)
-    side = lane // half
-    land(near[...], (plane ^ 3) * 2 + side)
-    for i, block in enumerate(direct):
-        at = pl.multiple_of(((lane % half) ^ i) * cap, cap)
-        stage[pl.ds(at, cap), :] = block[...]
-    columns = pl.multiple_of(((plane ^ 3) * 2 + 1 - side) * span, LANES)
-    out[:, pl.ds(columns, span)] = jnp.transpose(stage[...])[0:nodes, :]
+        for part in range(arrived.shape[0] // LANES):
+            at = (plane ^ apart) * (arrived.shape[0] // LANES) + part
+            tile = arrived[part * LANES:(part + 1) * LANES, :]
+            copies.append(land(tile, out, stage, sem, len(copies), at))
+    for copy in copies:
+        copy.wait()
+
+
+def last_kernel(devices, near, far, history, out, stage, sem):
+    me, plane, lane, lanes = whereabouts(devices)
+    side = lane // (lanes // 2)
+    first = land(near[...], out, stage, sem, 0, (plane ^ 3) * 2 + side)
+    second = land(far[...], out, stage, sem, 1, (plane ^ 3) * 2 + 1 - side)
+    first.wait()
+    second.wait()
 
 
 def back_kernel(at, *refs):
@@ -255,8 +262,8 @@
     out[...] = (dot(hi, serves) + dot(lo, serves))[0:out.shape[0], :]
 
 
-def params():
-    return pltpu.CompilerParams(vmem_limit_bytes=56 * 2**20)
+def params(mib=24):
+    return pltpu.CompilerParams(vmem_limit_bytes=mib * 2**20)
 
 
 def shards(
@@ -287,11 +294,12 @@
         in_specs=[vmem] * 6 + [smem] + [vmem] * 2,
         out_specs=[vmem] * 9,
         scratch_shapes=[pltpu.VMEM((rows, deep), f32), pltpu.VMEM((8, columns), f32)],
-        compiler_params=params(),
+        compiler_params=params(40),
     )(new_owner.reshape(1, columns), qp_to_rve, history, yield_flags, strain, stiffness, pattern,
       coupling, plastic_dir)
 
     chunks = columns // LANES
+    small = pl.CostEstimate(flops=2**10, bytes_accessed=2**10, transcendentals=0)
     lanes = devices // PLANES
     half = lanes // 2
     wide = comps * LANES
@@ -300,7 +308,9 @@
     updated, stress_s, ready = [], [], []
     for k in range(chunks):
         part = lambda height: pl.BlockSpec((height, LANES), lambda i, k=k: (0, k))
-        outs = [block(half * per_peer)] if k < 3 else [block(per_peer)] * half
+        outs = [block(LANES)]
+        if k == chunks - 1:
+            outs = [block(LANES)] * 3
         done = pl.pallas_call(
             functools.partial(solve_kernel, 1.0 / math.sqrt(comps * nodes), k * LANES, k),
             grid=(1,),
@@ -316,22 +326,18 @@
             scratch_shapes=[pltpu.VMEM((rows, wide), f32) for _ in range(4)]
             + [pltpu.VMEM((deep, 2 * wide), bf16)],
             compiler_params=params(),
-            cost_estimate=pl.CostEstimate(
-                flops=18 * rows * deep * wide, bytes_accessed=8 * 2**20, transcendentals=0
-            ),
+            cost_estimate=small,
         )(khi, klo, hist_s, weight_s, strain_s, cstack, pdir, place_s, *updated)
         updated.append(done[0])
         stress_s.append(done[1])
         ready.append(done[2:])
-    last = pl.pallas_call(
-        functools.partial(ship_kernel, chunks * LANES, chunks),
-        out_shape=(block(lanes * per_peer),) * 2,
+    own_sent = pl.pallas_call(
+        functools.partial(ship_kernel, 6 * LANES, chunks),
+        out_shape=block(2 * LANES),
         in_specs=[vmem] * (1 + chunks),
-        out_specs=[vmem] * 2,
+        out_specs=vmem,
         compiler_params=params(),
-        cost_estimate=pl.CostEstimate(
-            flops=4 * rows * columns * columns, bytes_accessed=4 * 2**20, transcendentals=0
-        ),
+        cost_estimate=small,
     )(place_s, *updated)
 
     axes = ("macro", "pool")
@@ -348,23 +354,38 @@
         ).reshape(shape)
 
     two_a, two_b = hop(ready[0][0], 2 * lanes), hop(ready[1][0], 2 * lanes)
-    near = hop(ready[2][0], 3 * lanes)
-    direct = [hop(sent, 3 * lanes + half + i) for i, sent in enumerate(ready[3])]
-    one = hop(last[0], lanes)
-    two_a, two_b, own = lax.optimization_barrier((two_a, two_b, last[1]))
-    own = spread(own, lanes)
+    one_a, one_b = hop(ready[2][0], lanes), hop(ready[3][0], lanes)
+    near = hop(ready[3][1], 3 * lanes)
+    far = hop(ready[3][2], 3 * lanes + half)
+    two_a, two_b, _ = lax.optimization_barrier((two_a, two_b, updated[3]))
     two = spread(jnp.concatenate([two_a, two_b], axis=0), lanes)
-    near, two, own = lax.optimization_barrier((near, two, own))
+    own = spread(own_sent, lanes)
+    one_a, one_b, near, _ = lax.optimization_barrier((one_a, one_b, near, own_sent))
+    one = spread(jnp.concatenate([one_a, one_b], axis=0), lanes)
     near = spread(near, half)
-    one = spread(one, lanes)
+    far, _, _ = lax.optimization_barrier((far, near, one))
+    far = spread(far, half)
+    hbm = pl.BlockSpec(memory_space=pl.ANY)
+    history_shape = jax.ShapeDtypeStruct((nodes, devices * per_peer), f32)
     new_history = pl.pallas_call(
-        functools.partial(land_kernel, devices, per_peer),
-        out_shape=jax.ShapeDtypeStruct((nodes, devices * per_peer), f32),
-        in_specs=[vmem] * (4 + half),
-        out_specs=vmem,
-        scratch_shapes=[pltpu.VMEM((LANES, deep), f32)],
+        functools.partial(land_kernel, devices),
+        out_shape=history_shape,
+        in_specs=[vmem] * 3,
+        out_specs=hbm,
+        scratch_shapes=[pltpu.VMEM((6, nodes, LANES), f32), pltpu.SemaphoreType.DMA((6,))],
         compiler_params=params(),
-    )(two, near, one, own, *direct)
+        cost_estimate=small,
+    )(two, one, own)
+    new_history = pl.pallas_call(
+        functools.partial(last_kernel, devices),
+        out_shape=history_shape,
+        in_specs=[vmem, vmem, hbm],
+        out_specs=hbm,
+        scratch_shapes=[pltpu.VMEM((2, nodes, LANES), f32), pltpu.SemaphoreType.DMA((2,))],
+        input_output_aliases={2: 0},
+        compiler_params=params(),
+        cost_estimate=small,
+    )(near, far, new_history)
     stress_out = pl.pallas_call(
         back_kernel,
         out_shape=jax.ShapeDtypeStruct((voigt, columns), f32),

time: 154 us -> 174 us (1.13)
  waiting for transfers between devices: 42.2 us -> 85.6 us
  Pallas kernels: 64.6 us -> 42.4 us
  blocking collectives: 16.6 us -> 0 us
  local copies, waits for them, and re-layouts: 0.94 us -> 9.94 us
  other arithmetic: 0.05 us -> 3 us
  starting transfers between devices: 28.6 us -> 31.2 us
    ppermute x8 -> x6, waiting for transfers between devices: 32 us -> 73.9 us  [hop(): return lax.ppermute(sent, axes, [(s, s ^ mask) for s in range(devices)])]
    all_to_all x1 -> x0, blocking collectives: 16.6 us -> none  [spread(): lax.all_to_all(sent.reshape(size, per_peer, deep), axes, split_axis=0, co...]
    pallas_call x4, Pallas kernels: 46.1 us -> 33.4 us  [shards(): pl.pallas_call(functools.partial(solve_kernel, 1.0 / math.sqrt(comps * no...]
    unnamed x26 -> x20, local copies, waits for them, and re-layouts: 0.94 us -> 9.94 us
    all_to_all x3 -> x5, starting transfers between devices: 10.6 us -> 19.5 us  [spread(): lax.all_to_all(sent.reshape(size, per_peer, deep), axes, split_axis=0, co...]
    ppermute x8 -> x6, starting transfers between devices: 18 us -> 11.7 us  [hop(): return lax.ppermute(sent, axes, [(s, s ^ mask) for s in range(devices)])]
    pallas_call x1, Pallas kernels: 8.28 us -> 3.62 us  [shards(): pl.pallas_call(functools.partial(prep_kernel, devices, per_peer), out_sha...]
    pallas_call x2 -> x3, Pallas kernels: 8.57 us -> 4.52 us  [the longest x1 1.88 us: shards(): pl.pallas_call(functools.partial(ship_kernel, 6 * LANES, chunks), out_sha...]
  transfers between devices with their start and end apart: 11 -> 11, of which waited for: 6 -> 9; matrix products, arithmetic and copies ran while one was open for 0% -> 2% of each run, Pallas kernels for 27% -> 1%
where the time goes in v1:
time: 174 us; the launch traced here: 173 us
  waiting for transfers between devices  85.6 us (49%)
  Pallas kernels  42.4 us (24%)
  starting transfers between devices  31.2 us (18%)
  local copies, waits for them, and re-layouts  9.94 us (6%)
  other arithmetic  3 us (2%)
    ppermute x6, waiting for transfers between devices, hop(): return lax.ppermute(sent, axes, [(s, s ^ mask) for s in range(devices)])  73.9 us
    pallas_call x4, Pallas kernels, shards(): pl.pallas_call(functools.partial(solve_kernel, 1.0 / math.sqrt(comps * no...  33.4 us
    all_to_all x5, starting transfers between devices, spread(): lax.all_to_all(sent.reshape(size, per_peer, deep), axes, split_axis=0, co...  19.5 us
    all_to_all x5, waiting for transfers between devices, spread(): lax.all_to_all(sent.reshape(size, per_peer, deep), axes, split_axis=0, co...  11.7 us
    ppermute x6, starting transfers between devices, hop(): return lax.ppermute(sent, axes, [(s, s ^ mask) for s in range(devices)])  11.7 us
    unnamed x20, local copies, waits for them, and re-layouts  9.94 us
    pallas_call x1, Pallas kernels, shards(): pl.pallas_call(functools.partial(prep_kernel, devices, per_peer), out_sha...  3.62 us
  transfers between devices with their start and end apart: 11, of which 9 were waited for; matrix products, arithmetic and copies ran while one was open for 2% of the time, Pallas kernels for 1%

profile of v1, /device:TPU:0, one launch (start us, length us, event | category | flops | bytes accessed | tf_op | source)
XLA Modules:
  0.0 173.0 jit_solution(4686821217254588409)
XLA Ops:
  0.6 2.0 %copy-done = f32[9,9,81,81]{3,2,1,0:T(8,128)S(1)} copy-done((f32[9,9,81,81]{3,2,1,0:T(8,128)S(1)}, f32[9,9,81,81]{3,2,1,0:T(8,128)}, u32[]{:S(2)}) %copy-start) | copy-done | bytes 2125788
  9.8 3.6 %shard_map.104 = (bf16[736,768]{1,0:T(8,128)(2,1)S(1)}, bf16[736,768]{1,0:T(8,128)(2,1)S(1)}, f32[736,512]{1,0:T(8,128)S(1)}, f32[736,512]{1,0:T(8,128)S(1)}, f3...) custom-call(s32[1,512]{1,0:T(1,128)S(1)} %bitcast.16, ...), custom_call_target="tpu_custom_call" | custom-call | tf_op jit(solution)/shard_map/pallas_call | solution.py:281
  13.4 8.0 %shard_map.105 = (f32[736,128]{1,0:T(8,128)S(1)}, f32[8,128]{1,0:T(8,128)S(1)}, f32[128,768]{1,0:T(8,128)S(1)}) custom-call(bf16[736,768]{1,0:T(8,128)(2,1)S(1)} %get-tuple-element.31.khi, bf16[736,768]{1,0:T(8,128)(2,1)S(1)} %get-tuple-element.32.klo, f32[736,512]{1,0:T(8,128)S(1)} %get-tuple-element.33.hist, f32[736,512]{1,0:T(8,128)S(1)} %get-tuple-element.34.weight, ...), custom_call_target="tpu_custom_call" | custom-call | flops 1024 | bytes 1024 | tf_op jit(solution)/shard_map/pallas_call | solution.py:314
  21.5 8.1 %shard_map.106 = (f32[736,128]{1,0:T(8,128)S(1)}, f32[8,128]{1,0:T(8,128)S(1)}, f32[128,768]{1,0:T(8,128)S(1)}) custom-call(bf16[736,768]{1,0:T(8,128)(2,1)S(1)} %get-tuple-element.31.khi, bf16[736,768]{1,0:T(8,128)(2,1)S(1)} %get-tuple-element.32.klo, f32[736,512]{1,0:T(8,128)S(1)} %get-tuple-element.33.hist, f32[736,512]{1,0:T(8,128)S(1)} %get-tuple-element.34.weight, ...), custom_call_target="tpu_custom_call" | custom-call | flops 1024 | bytes 1024 | tf_op jit(solution)/shard_map/pallas_call | solution.py:314
  29.6 8.3 %shard_map.107 = (f32[736,128]{1,0:T(8,128)S(1)}, f32[8,128]{1,0:T(8,128)S(1)}, f32[128,768]{1,0:T(8,128)S(1)}) custom-call(bf16[736,768]{1,0:T(8,128)(2,1)S(1)} %get-tuple-element.31.khi, bf16[736,768]{1,0:T(8,128)(2,1)S(1)} %get-tuple-element.32.klo, f32[736,512]{1,0:T(8,128)S(1)} %get-tuple-element.33.hist, f32[736,512]{1,0:T(8,128)S(1)} %get-tuple-element.34.weight, ...), custom_call_target="tpu_custom_call" | custom-call | flops 1024 | bytes 1024 | tf_op jit(solution)/shard_map/pallas_call | solution.py:314
  38.0 8.8 %shard_map.108 = (f32[736,128]{1,0:T(8,128)S(1)}, f32[8,128]{1,0:T(8,128)S(1)}, f32[128,768]{1,0:T(8,128)S(1)}, f32[128,768]{1,0:T(8,128)S(1)}, f32[128,768]{1,0:T(8,128)S(1)}) custom-call(bf16[736,768]{1,0:T(8,128)(2,1)S(1)} %get-tuple-element.31.khi, bf16[736,768]{1,0:T(8,128)(2,1)S(1)} %get-tuple-element.32.klo, f32[736,512]{1,0:T(8,128)S(1)} %get-tuple-element.33.hist, ...), custom_call_target="tpu_custom_call" | custom-call | flops 1024 | bytes 1024 | tf_op jit(solution)/shard_map/pallas_call | solution.py:314
  46.8 1.9 %shard_map.109 = f32[256,768]{1,0:T(8,128)} custom-call(s32[8,512]{1,0:T(8,128)S(1)} %get-tuple-element.38.place, f32[736,128]{1,0:T(8,128)S(1)} %get-tuple-element.39.refs_0_, f32[736,128]{1,0:T(8,128)S(1)} %get-tuple-element.40.refs_1_, f32[736,128]{1,0:T(8,128)S(1)} %get-tuple-element.42.refs_2_, f32[736,128]{1,0:T(8,128)S(1)} %get-tuple-element.45.refs_3_), custom_call_target="tpu_custom_call" | custom-call | flops 1024 | bytes 1024 | tf_op jit(solution)/shard_map/pallas_call | solution.py:334
  48.7 5.2 %all-to-all-start.4 = ((f32[8,32,768]{2,1,0:T(8,128)}), f32[8,32,768]{2,1,0:T(8,128)S(1)}, u32[]{:S(2)}, u32[]{:S(2)}) async-start(f32[8,32,768]{2,1,0:T(8,128)} %bitcast.9), calls=%async_computation.4 | async-start | bytes 1572864 | tf_op jit(solution)/shard_map/all_to_all | solution.py:351
  55.9 3.6 %collective-permute-start.2 = (f32[128,768]{1,0:T(8,128)S(1)}, f32[128,768]{1,0:T(8,128)}, u32[]{:S(2)}, u32[]{:S(2)}) collective-permute-start(f32[128,768]{1,0:T(8,128)S(1)} %get-tuple-element.44), channel_id=1, source_target_pairs={{0,24},{1,25},{2,26},{3,27},{4,28},{5,29},{6,30},{7,31},{8,16},{9,... | collective-permute-start | bytes 1179656 | tf_op jit(solution)/shard_map/ppermute | solution.py:346
  59.5 6.4 %collective-permute-done = f32[128,768]{1,0:T(8,128)} collective-permute-done((f32[128,768]{1,0:T(8,128)S(1)}, f32[128,768]{1,0:T(8,128)}, u32[]{:S(2)}, u32[]{:S(2)}) %collective-permute-start) | collective-permute-done | bytes 393248 | tf_op jit(solution)/shard_map/ppermute | solution.py:346
  65.9 7.9 %collective-permute-done.1 = f32[128,768]{1,0:T(8,128)S(1)} collective-permute-done((f32[128,768]{1,0:T(8,128)S(1)}, f32[128,768]{1,0:T(8,128)S(1)}, u32[]{:S(2)}, u32[]{:S(2)}) %collective-permute-start.1) | collective-permute-done | bytes 393248 | tf_op jit(solution)/shard_map/ppermute | solution.py:346
  74.6 9.8 %collective-permute-done.2 = f32[128,768]{1,0:T(8,128)} collective-permute-done((f32[128,768]{1,0:T(8,128)S(1)}, f32[128,768]{1,0:T(8,128)}, u32[]{:S(2)}, u32[]{:S(2)}) %collective-permute-start.2) | collective-permute-done | bytes 393248 | tf_op jit(solution)/shard_map/ppermute | solution.py:346
  84.4 3.5 %all-to-all-start = ((f32[4,32,768]{2,1,0:T(8,128)}), f32[4,32,768]{2,1,0:T(8,128)S(1)}, u32[]{:S(2)}, u32[]{:S(2)}) async-start(f32[4,32,768]{2,1,0:T(8,128)} %bitcast.1), calls=%async_computation | async-start | bytes 786432 | tf_op jit(solution)/shard_map/all_to_all | solution.py:351
  87.8 2.1 %pad_maximum_fusion = f32[256,768]{1,0:T(8,128)} fusion(f32[128,768]{1,0:T(8,128)} %copy-done.9, f32[128,768]{1,0:T(8,128)} %collective-permute-done), kind=kLoop, calls=%fused_computation | loop fusion | flops 196608 | bytes 1572864 | tf_op jit(solution)/shard_map/concatenate | solution.py:364
  89.9 5.3 %all-to-all-done = f32[4,32,768]{2,1,0:T(8,128)S(1)} async-done(((f32[4,32,768]{2,1,0:T(8,128)}), f32[4,32,768]{2,1,0:T(8,128)S(1)}, u32[]{:S(2)}, u32[]{:S(2)}) %all-to-all-start) | async-done | bytes 393248 | tf_op jit(solution)/shard_map/all_to_all | solution.py:351
  95.3 3.5 %all-to-all-start.1 = ((f32[8,32,768]{2,1,0:T(8,128)}), f32[8,32,768]{2,1,0:T(8,128)S(1)}, u32[]{:S(2)}, u32[]{:S(2)}) async-start(f32[8,32,768]{2,1,0:T(8,128)} %bitcast.17), calls=%async_computation.1 | async-start | bytes 1572864 | tf_op jit(solution)/shard_map/all_to_all | solution.py:351
  98.9 2.9 %collective-permute-start.5 = (f32[128,768]{1,0:T(8,128)S(1)}, f32[128,768]{1,0:T(8,128)S(1)}, u32[]{:S(2)}, u32[]{:S(2)}) collective-permute-start(f32[128,768]{1,0:T(8,128)S(1)} %get-tuple-element.52), channel_id=1, source_target_pairs={{0,16},{1,17},{2,18},{3,19},{4,20},{5,21},{6,22},{7,23},{8,24},{9,... | collective-permute-start | bytes 1179656 | tf_op jit(solution)/shard_map/ppermute | solution.py:346
  101.8 25.8 %collective-permute-done.4 = f32[128,768]{1,0:T(8,128)S(1)} collective-permute-done((f32[128,768]{1,0:T(8,128)S(1)}, f32[128,768]{1,0:T(8,128)S(1)}, u32[]{:S(2)}, u32[]{:S(2)}) %collective-permute-start.4) | collective-permute-done | bytes 393248 | tf_op jit(solution)/shard_map/ppermute | solution.py:346
  127.6 8.4 %collective-permute-done.5 = f32[128,768]{1,0:T(8,128)S(1)} collective-permute-done((f32[128,768]{1,0:T(8,128)S(1)}, f32[128,768]{1,0:T(8,128)S(1)}, u32[]{:S(2)}, u32[]{:S(2)}) %collective-permute-start.5) | collective-permute-done | bytes 393248 | tf_op jit(solution)/shard_map/ppermute | solution.py:346
  137.0 3.9 %all-to-all-start.3 = ((f32[8,32,768]{2,1,0:T(8,128)}), f32[8,32,768]{2,1,0:T(8,128)S(1)}, u32[]{:S(2)}, u32[]{:S(2)}) async-start(f32[8,32,768]{2,1,0:T(8,128)} %bitcast.18), calls=%async_computation.3 | async-start | bytes 1572864 | tf_op jit(solution)/shard_map/all_to_all | solution.py:351
  140.8 3.0 %collective-permute-start.3 = (f32[128,768]{1,0:T(8,128)S(1)}, f32[128,768]{1,0:T(8,128)}, u32[]{:S(2)}, u32[]{:S(2)}) collective-permute-start(f32[128,768]{1,0:T(8,128)S(1)} %get-tuple-element.47), channel_id=1, source_target_pairs={{0,28},{1,29},{2,30},{3,31},{4,24},{5,25},{6,26},{7,27},{8,20},{9,... | collective-permute-start | bytes 1179656 | tf_op jit(solution)/shard_map/ppermute | solution.py:346
  143.9 15.6 %collective-permute-done.3 = f32[128,768]{1,0:T(8,128)} collective-permute-done((f32[128,768]{1,0:T(8,128)S(1)}, f32[128,768]{1,0:T(8,128)}, u32[]{:S(2)}, u32[]{:S(2)}) %collective-permute-start.3) | collective-permute-done | bytes 393248 | tf_op jit(solution)/shard_map/ppermute | solution.py:346
  160.9 3.5 %all-to-all-start.2 = ((f32[4,32,768]{2,1,0:T(8,128)}), f32[4,32,768]{2,1,0:T(8,128)S(1)}, u32[]{:S(2)}, u32[]{:S(2)}) async-start(f32[4,32,768]{2,1,0:T(8,128)} %bitcast.5), calls=%async_computation.2 | async-start | bytes 786432 | tf_op jit(solution)/shard_map/all_to_all | solution.py:351
  166.9 4.9 %all-to-all-done.2 = f32[4,32,768]{2,1,0:T(8,128)S(1)} async-done(((f32[4,32,768]{2,1,0:T(8,128)}), f32[4,32,768]{2,1,0:T(8,128)S(1)}, u32[]{:S(2)}, u32[]{:S(2)}) %all-to-all-start.2) | async-done | bytes 393248 | tf_op jit(solution)/shard_map/all_to_all | solution.py:351
  (29 shorter events, 15.9 us)
Async XLA Ops:
  0.6 2.0 %copy-start = (f32[9,9,81,81]{3,2,1,0:T(8,128)S(1)}, f32[9,9,81,81]{3,2,1,0:T(8,128)}, u32[]{:S(2)}) copy-start(f32[9,9,81,81]{3,2,1,0:T(8,128)} %stiff.1) | copy-start | bytes 6377296
  2.7 1.4 copy-start.1
  4.1 1.4 copy-start.2
  5.4 0.9 copy-start.3
  6.3 0.7 copy-start.4
  7.0 0.7 copy-start.5
  7.7 0.7 copy-start.6
  8.4 0.7 copy-start.7
  9.1 0.7 copy-start.8
  48.7 35.7 %all-to-all-start.4 = ((f32[8,32,768]{2,1,0:T(8,128)}), f32[8,32,768]{2,1,0:T(8,128)S(1)}, u32[]{:S(2)}, u32[]{:S(2)}) async-start(f32[8,32,768]{2,1,0:T(8,128)} %bitcast.9), calls=%async_computation.4 | async-start | bytes 1572864 | tf_op jit(solution)/shard_map/all_to_all | solution.py:351
  53.9 12.0 %collective-permute-start = (f32[128,768]{1,0:T(8,128)S(1)}, f32[128,768]{1,0:T(8,128)}, u32[]{:S(2)}, u32[]{:S(2)}) collective-permute-start(f32[128,768]{1,0:T(8,128)S(1)} %get-tuple-element.41), channel_id=1, source_target_pairs={{0,8},{1,9},{2,10},{3,11},{4,12},{5,13},{6,14},{7,15},{8,0},{9,1},... | collective-permute-start | bytes 1179656 | tf_op jit(solution)/shard_map/ppermute | solution.py:346
  55.4 18.4 %collective-permute-start.1 = (f32[128,768]{1,0:T(8,128)S(1)}, f32[128,768]{1,0:T(8,128)S(1)}, u32[]{:S(2)}, u32[]{:S(2)}) collective-permute-start(f32[128,768]{1,0:T(8,128)S(1)} %get-tuple-element.43), channel_id=1, source_target_pairs={{0,8},{1,9},{2,10},{3,11},{4,12},{5,13},{6,14},{7,15},{8,0},{9,1},... | collective-permute-start | bytes 1179656 | tf_op jit(solution)/shard_map/ppermute | solution.py:346
  55.9 28.5 %collective-permute-start.2 = (f32[128,768]{1,0:T(8,128)S(1)}, f32[128,768]{1,0:T(8,128)}, u32[]{:S(2)}, u32[]{:S(2)}) collective-permute-start(f32[128,768]{1,0:T(8,128)S(1)} %get-tuple-element.44), channel_id=1, source_target_pairs={{0,24},{1,25},{2,26},{3,27},{4,28},{5,29},{6,30},{7,31},{8,16},{9,... | collective-permute-start | bytes 1179656 | tf_op jit(solution)/shard_map/ppermute | solution.py:346
  73.8 0.8 copy-start.9
  84.4 10.9 %all-to-all-start = ((f32[4,32,768]{2,1,0:T(8,128)}), f32[4,32,768]{2,1,0:T(8,128)S(1)}, u32[]{:S(2)}, u32[]{:S(2)}) async-start(f32[4,32,768]{2,1,0:T(8,128)} %bitcast.1), calls=%async_computation | async-start | bytes 786432 | tf_op jit(solution)/shard_map/all_to_all | solution.py:351
  95.3 41.7 %all-to-all-start.1 = ((f32[8,32,768]{2,1,0:T(8,128)}), f32[8,32,768]{2,1,0:T(8,128)S(1)}, u32[]{:S(2)}, u32[]{:S(2)}) async-start(f32[8,32,768]{2,1,0:T(8,128)} %bitcast.17), calls=%async_computation.1 | async-start | bytes 1572864 | tf_op jit(solution)/shard_map/all_to_all | solution.py:351
  98.8 28.8 %collective-permute-start.4 = (f32[128,768]{1,0:T(8,128)S(1)}, f32[128,768]{1,0:T(8,128)S(1)}, u32[]{:S(2)}, u32[]{:S(2)}) collective-permute-start(f32[128,768]{1,0:T(8,128)S(1)} %get-tuple-element.51), channel_id=1, source_target_pairs={{0,16},{1,17},{2,18},{3,19},{4,20},{5,21},{6,22},{7,23},{8,24},{9,... | collective-permute-start | bytes 1179656 | tf_op jit(solution)/shard_map/ppermute | solution.py:346
  98.9 37.1 %collective-permute-start.5 = (f32[128,768]{1,0:T(8,128)S(1)}, f32[128,768]{1,0:T(8,128)S(1)}, u32[]{:S(2)}, u32[]{:S(2)}) collective-permute-start(f32[128,768]{1,0:T(8,128)S(1)} %get-tuple-element.52), channel_id=1, source_target_pairs={{0,16},{1,17},{2,18},{3,19},{4,20},{5,21},{6,22},{7,23},{8,24},{9,... | collective-permute-start | bytes 1179656 | tf_op jit(solution)/shard_map/ppermute | solution.py:346
  137.0 24.0 %all-to-all-start.3 = ((f32[8,32,768]{2,1,0:T(8,128)}), f32[8,32,768]{2,1,0:T(8,128)S(1)}, u32[]{:S(2)}, u32[]{:S(2)}) async-start(f32[8,32,768]{2,1,0:T(8,128)} %bitcast.18), calls=%async_computation.3 | async-start | bytes 1572864 | tf_op jit(solution)/shard_map/all_to_all | solution.py:351
  140.8 18.6 %collective-permute-start.3 = (f32[128,768]{1,0:T(8,128)S(1)}, f32[128,768]{1,0:T(8,128)}, u32[]{:S(2)}, u32[]{:S(2)}) collective-permute-start(f32[128,768]{1,0:T(8,128)S(1)} %get-tuple-element.47), channel_id=1, source_target_pairs={{0,28},{1,29},{2,30},{3,31},{4,24},{5,25},{6,26},{7,27},{8,20},{9,... | collective-permute-start | bytes 1179656 | tf_op jit(solution)/shard_map/ppermute | solution.py:346
  160.9 10.9 %all-to-all-start.2 = ((f32[4,32,768]{2,1,0:T(8,128)}), f32[4,32,768]{2,1,0:T(8,128)S(1)}, u32[]{:S(2)}, u32[]{:S(2)}) async-start(f32[4,32,768]{2,1,0:T(8,128)} %bitcast.5), calls=%async_computation.2 | async-start | bytes 786432 | tf_op jit(solution)/shard_map/all_to_all | solution.py:351

commit v2 on v1

v2 whole, which is shorter than its diff:
```python
import functools
import math

import jax
import jax.numpy as jnp
from jax import lax
from jax.experimental import pallas as pl
from jax.experimental.pallas import tpu as pltpu
from jax.sharding import PartitionSpec as P

ITERS = 3
LANES = 128
PLANES = 4

NN = (((1,), (0,)), ((), ()))
NT = (((1,), (1,)), ((), ()))
TN = (((0,), (0,)), ((), ()))


def up(value, unit):
    return -(-value // unit) * unit


def dot(a, b, dims=NN):
    return lax.dot_general(a, b, dims, preferred_element_type=jnp.float32)


def halves(x):
    hi = x.astype(jnp.bfloat16)
    lo = (x - hi.astype(jnp.float32)).astype(jnp.bfloat16)
    return hi, lo


def whereabouts(devices):
    me = lax.axis_index("macro") * lax.axis_size("pool") + lax.axis_index("pool")
    lanes = devices // PLANES
    return me, me // lanes, me % lanes, lanes


def hot(row, count):
    rows = lax.broadcasted_iota(jnp.int32, (count, row.shape[1]), 0)
    return jnp.where(rows == row, 1.0, 0.0).astype(jnp.bfloat16)


def prep_kernel(devices, per_peer, *refs):
    sources, outs, (kfull, pad), local, sem = refs[:9], refs[9:18], refs[18:20], refs[20:29], refs[29]
    khi, klo, hist_s, weight_s, strain_s, place_s, qp_s, cstack, pdir = outs
    owner, qp, strain, stiff, pattern, hist, flag, coupling, plastic = local
    copies = [
        pltpu.make_async_copy(source, target, sem.at[i])
        for i, (source, target) in enumerate(zip(sources, local))
    ]
    for copy in copies:
        copy.start()
    nodes, columns = hist.shape
    nb, blk = stiff.shape[0], stiff.shape[2]
    comps, voigt = coupling.shape[0], coupling.shape[1]

    me, plane, lane, lanes = whereabouts(devices)
    for copy in copies[:3]:
        copy.wait()
    apart = owner[...] // lanes ^ plane
    target = owner[...] % lanes
    turn = jnp.where(apart == 2, 0, jnp.where(apart == 3, 1, jnp.where(apart == 1, 2, 3)))
    key = turn * lanes + jnp.where(apart >= 2, target, target ^ lane)
    key_ids = lax.broadcasted_iota(jnp.int32, (devices, columns), 0)
    mine = jnp.where(key_ids == key, 1.0, 0.0)
    earlier = jnp.where(
        lax.broadcasted_iota(jnp.int32, (columns, columns), 0)
        < lax.broadcasted_iota(jnp.int32, (columns, columns), 1), 1.0, 0.0
    ).astype(jnp.bfloat16)
    before = dot(mine.astype(jnp.bfloat16), earlier)
    rank = jnp.sum(before * mine, axis=0, keepdims=True)
    tally = jnp.sum(mine, axis=1, keepdims=True)
    ahead = jnp.where(key_ids < key, tally, 0.0)
    position = (rank + jnp.sum(ahead, axis=0, keepdims=True)).astype(jnp.int32)

    order = hot(position, columns)
    pad[...] = jnp.zeros_like(pad)
    pad[0:1, :] = key.astype(jnp.float32)
    pad[1:2, :] = rank
    placed = dot(pad[...].astype(jnp.bfloat16), order, NT)
    place_s[...] = jnp.broadcast_to(
        (placed[0:1, :] * per_peer + placed[1:2, :]).astype(jnp.int32), place_s.shape
    )

    pad[0:1, :] = (position // 256).astype(jnp.float32)
    pad[1:2, :] = (position % 256).astype(jnp.float32)
    found = dot(pad[...].astype(jnp.bfloat16), hot(qp[...], columns))
    at = (found[0:1, :] * 256.0 + found[1:2, :]).astype(jnp.int32)
    qp_s[...] = jnp.broadcast_to(at, qp_s.shape)
    pad[...] = jnp.zeros_like(pad)
    pad[0:voigt, :] = strain[...]
    hi, lo = halves(pad[...])
    serves = hot(at, columns)
    strain_s[...] = dot(hi, serves, NT) + dot(lo, serves, NT)

    kfull[...] = jnp.zeros_like(kfull)
    copies[3].wait()
    copies[4].wait()
    for a in range(nb):
        for b in range(nb):
            kfull[a * blk:(a + 1) * blk, b * blk:(b + 1) * blk] = (
                stiff[a, b] * pattern[a, b].astype(jnp.float32)
            )
    k = kfull[...]
    kh = k.astype(jnp.bfloat16)
    khi[...] = kh
    klo[...] = (k - kh.astype(jnp.float32)).astype(jnp.bfloat16)

    copies[5].wait()
    copies[6].wait()
    hi, lo = halves(hist[...])
    hist_s[...] = jnp.zeros_like(hist_s)
    hist_s[0:nodes, :] = dot(hi, order, NT) + dot(lo, order, NT)
    h = hist_s[...]
    weight_s[...] = jnp.zeros_like(weight_s)
    weight_s[0:nodes, :] = dot(flag[...].astype(jnp.float32).astype(jnp.bfloat16), order, NT)
    weight_s[...] = weight_s[...] * h * h / (1.0 + h * h)

    copies[7].wait()
    copies[8].wait()
    cstack[...] = jnp.zeros_like(cstack)
    for c in range(comps):
        cpl = coupling[c]
        hi = cpl.astype(jnp.bfloat16).astype(jnp.float32)
        cstack[c, 0:voigt, 0:nodes] = hi
        cstack[c, 8:8 + voigt, 0:nodes] = hi
        cstack[c, 16:16 + voigt, 0:nodes] = cpl - hi
    pdir[...] = jnp.zeros_like(pdir)
    for c in range(comps):
        spread = jnp.broadcast_to(plastic[c:c + 1, :], (LANES, nodes))
        pdir[c, 0:nodes, :] = jnp.transpose(spread)


def sweep(rows, comps, span):
    pieces = 4 * span // LANES
    cuts = [rows // 16 * i // pieces * 16 for i in range(pieces + 1)]
    for top, end in zip(cuts, cuts[1:]):
        for c in range(comps):
            yield slice(top, end), slice(c * span, (c + 1) * span), c


def fold(x):
    return jnp.sum(x.reshape(x.shape[0] // 8, 8, x.shape[1]), axis=0)


def total(parts):
    return jnp.sum(parts, axis=0, keepdims=True)


def solve_kernel(scale, first, earlier, khi, klo, hist, weight, strain, cstack, pdir, place, *refs):
    earlier_updated, refs = refs[:earlier], refs[earlier:]
    updated, stress, blocks = refs[0], refs[1], refs[2:-5]
    field, resid, image, solved, split = refs[-5:]
    rows, span = hist.shape
    comps = pdir.shape[0]
    wide = comps * span
    zero = jnp.zeros((8, span), jnp.float32)

    def flow(c, r):
        return jnp.concatenate([pdir[c, r, :]] * (span // LANES), axis=1)

    def keep(r, c, x):
        split[r, c * span:(c + 1) * span], split[r, wide + c * span:wide + (c + 1) * span] = (
            halves(x)
        )

    s = strain[...]
    s_hi = s.astype(jnp.bfloat16).astype(jnp.float32)
    s3 = jnp.concatenate([s_hi, s - s_hi, s_hi, jnp.zeros_like(s)], axis=0).astype(jnp.bfloat16)
    split[rows:, :] = jnp.zeros((split.shape[0] - rows, 2 * wide), jnp.bfloat16)
    for c in range(comps):
        image[:, c * span:(c + 1) * span] = dot(cstack[c].astype(jnp.bfloat16), s3, TN)
    parts = zero
    for r, l, c in sweep(rows, comps, span):
        d = image[r, l] - weight[r, :] * hist[r, :] * flow(c, r)
        resid[r, l] = d
        field[r, l] = d
        keep(r, c, d)
        parts = parts + fold(d * d)
    norm = total(parts)
    for step in range(ITERS):
        both = dot(khi[...], split[...])
        image[...] = both[:, 0:wide] + both[:, wide:] + dot(klo[...], split[:, 0:wide])
        parts = zero
        for r, l, c in sweep(rows, comps, span):
            d = field[r, l]
            q = image[r, l] + (1.5 - weight[r, :]) * d
            image[r, l] = q
            parts = parts + fold(d * q)
        alpha = norm / jnp.maximum(total(parts), 1.0)
        if step == ITERS - 1:
            break
        parts = zero
        for r, l, c in sweep(rows, comps, span):
            gain = alpha * field[r, l]
            solved[r, l] = gain if step == 0 else solved[r, l] + gain
            left = resid[r, l] - alpha * image[r, l]
            resid[r, l] = left
            parts = parts + fold(left * left)
        following = total(parts)
        beta = following / jnp.maximum(norm, 1.0)
        norm = following
        for r, l, c in sweep(rows, comps, span):
            d = resid[r, l] + beta * field[r, l]
            field[r, l] = d
            keep(r, c, d)
    for r, l, c in sweep(rows, comps, span):
        x = solved[r, l] + alpha * field[r, l]
        pushed = flow(c, r) * x
        image[r, 0:span] = pushed if c == 0 else image[r, 0:span] + pushed
        keep(r, c, (1.5 - weight[r, :]) * x)
    updated[...] = hist[...] + weight[...] * image[:, 0:span]
    if blocks:
        place_blocks(first, place, [*earlier_updated, updated], blocks)
    out = s
    for c in range(comps):
        cpl = cstack[c].astype(jnp.bfloat16)
        main = dot(cpl, split[0:rows, c * span:(c + 1) * span])
        minor = dot(cpl, split[0:rows, wide + c * span:wide + (c + 1) * span])
        out = out + scale * (main[0:8] + main[16:24] + minor[0:8])
    stress[...] = out


def place_blocks(first, place, sources, blocks):
    rows = sources[0].shape[0]
    count = sum(block.shape[0] for block in blocks)
    width = sum(source.shape[1] for source in sources)
    placing = hot(place[0:1, 0:width] - first, count)
    sums, left = 0.0, 0
    for source in sources:
        hi, lo = halves(source[...])
        cut = placing[:, left:left + source.shape[1]]
        sums = sums + (dot(cut, hi, NT) + dot(cut, lo, NT))
        left += source.shape[1]
    top = 0
    for block in blocks:
        block[:, 0:rows] = sums[top:top + block.shape[0], :]
        block[:, rows:] = jnp.zeros((block.shape[0], block.shape[1] - rows), jnp.float32)
        top += block.shape[0]


def ship_kernel(first, chunks, place, *refs):
    place_blocks(first, place, refs[:chunks], refs[chunks:])


def land(tile, out, stage, sem, slot, at):
    nodes = out.shape[0]
    stage[slot] = jnp.transpose(tile)[0:nodes, :]
    columns = pl.multiple_of(at * LANES, LANES)
    copy = pltpu.make_async_copy(stage.at[slot], out.at[:, pl.ds(columns, LANES)], sem.at[slot])
    copy.start()
    return copy


def land_group(block, count, plane, out, stage, sem, slot):
    height = block.shape[0] // count
    copies = []
    for part in range(count):
        tile = block[part * height:(part + 1) * height, :]
        copies.append(land(tile, out, stage, sem, slot + part, plane * count + part))
    return copies


def land_kernel(devices, cap, *refs):
    blocks, (out, stage, sem, gather) = refs[:-4], refs[-4:]
    me, plane, lane, lanes = whereabouts(devices)
    copies = []
    for apart in range(2):
        for i in range(lanes):
            at = pl.multiple_of((lane ^ i) * cap, cap)
            gather[apart, pl.ds(at, cap), :] = blocks[apart * lanes + i][...]
        copies += land_group(gather.at[apart], 2, plane ^ apart, out, stage, sem, 2 * apart)
    for copy in copies:
        copy.wait()


def last_kernel(devices, pair, history, out, stage, sem):
    me, plane, lane, lanes = whereabouts(devices)
    group = pair.shape[0] // 2
    copies = []
    for part in range(2):
        mine = (plane // 2) == part
        source = jnp.where(mine, plane ^ 2, plane ^ 3)
        block = pair.at[part * group:(part + 1) * group, :]
        copies += land_group(block, 2, source, out, stage, sem, 2 * part)
    for copy in copies:
        copy.wait()


def back_kernel(at, *refs):
    out = refs[-1]
    stress = jnp.concatenate([ref[...] for ref in refs[:-1]], axis=1)
    serves = hot(at[0:1, :], stress.shape[1])
    hi, lo = halves(stress)
    out[...] = (dot(hi, serves) + dot(lo, serves))[0:out.shape[0], :]


def params(mib=24):
    return pltpu.CompilerParams(vmem_limit_bytes=mib * 2**20)


def shards(
    history, yield_flags, strain, qp_to_rve, new_owner, stiffness, pattern, coupling, plastic_dir
):
    devices = lax.axis_size(("macro", "pool"))
    nodes, columns = history.shape
    comps, voigt = coupling.shape[0], coupling.shape[1]
    per_peer = 2 * columns // devices
    rows = up(nodes, 32)
    deep = up(nodes, 256)
    f32, bf16, i32 = jnp.float32, jnp.bfloat16, jnp.int32
    vmem = pl.BlockSpec(memory_space=pltpu.VMEM)
    inputs = (new_owner.reshape(1, columns), qp_to_rve, strain, stiffness, pattern, history,
              yield_flags, coupling, plastic_dir)
    khi, klo, hist_s, weight_s, strain_s, place_s, qp_s, cstack, pdir = pl.pallas_call(
        functools.partial(prep_kernel, devices, per_peer),
        out_shape=(
            jax.ShapeDtypeStruct((rows, deep), bf16),
            jax.ShapeDtypeStruct((rows, deep), bf16),
            jax.ShapeDtypeStruct((rows, columns), f32),
            jax.ShapeDtypeStruct((rows, columns), f32),
            jax.ShapeDtypeStruct((8, columns), f32),
            jax.ShapeDtypeStruct((8, columns), i32),
            jax.ShapeDtypeStruct((8, columns), i32),
            jax.ShapeDtypeStruct((comps, 32, rows), f32),
            jax.ShapeDtypeStruct((comps, rows, LANES), f32),
        ),
        in_specs=[pl.BlockSpec(memory_space=pltpu.HBM)] * 9,
        out_specs=[vmem] * 9,
        scratch_shapes=[pltpu.VMEM((rows, deep), f32), pltpu.VMEM((8, columns), f32)]
        + [(pltpu.SMEM if x is pattern else pltpu.VMEM)(x.shape, x.dtype) for x in inputs]
        + [pltpu.SemaphoreType.DMA((9,))],
        compiler_params=params(46),
    )(*inputs)

    lanes = devices // PLANES
    group = lanes * per_peer
    block = lambda height: jax.ShapeDtypeStruct((height, deep), f32)
    whole = lambda shape: pl.BlockSpec(shape, lambda i: (0,) * len(shape))
    updated, stress_s, ready = [], [], []
    left = 0
    for span in (LANES, LANES, columns - 2 * LANES):
        part = lambda height: pl.BlockSpec((height, span), lambda i, at=left // span: (0, at))
        wide = comps * span
        outs = [block(LANES)] if len(updated) < 2 else []
        done = pl.pallas_call(
            functools.partial(solve_kernel, 1.0 / math.sqrt(comps * nodes), left, len(updated)),
            grid=(1,),
            out_shape=(
                jax.ShapeDtypeStruct((rows, span), f32),
                jax.ShapeDtypeStruct((8, span), f32),
                *outs,
            ),
            in_specs=[whole((rows, deep)), whole((rows, deep)), part(rows), part(rows), part(8),
                      whole((comps, 32, rows)), whole((comps, rows, LANES)), whole((8, columns))]
            + [whole(u.shape) for u in updated],
            out_specs=[whole((rows, span)), whole((8, span))] + [whole(o.shape) for o in outs],
            scratch_shapes=[pltpu.VMEM((rows, wide), f32) for _ in range(4)]
            + [pltpu.VMEM((deep, 2 * wide), bf16)],
            compiler_params=params(28),
            cost_estimate=pl.CostEstimate(
                flops=2 * rows * deep * wide, bytes_accessed=2**20, transcendentals=0
            ),
        )(khi, klo, hist_s, weight_s, strain_s, cstack, pdir, place_s, *updated)
        updated.append(done[0])
        stress_s.append(done[1])
        ready.extend(done[2:])
        left += span
    three, *singles = pl.pallas_call(
        functools.partial(ship_kernel, group, len(updated)),
        out_shape=(block(group),) + (block(per_peer),) * (2 * lanes),
        in_specs=[vmem] * (1 + len(updated)),
        out_specs=[vmem] * (1 + 2 * lanes),
        compiler_params=params(28),
        cost_estimate=pl.CostEstimate(
            flops=2**20, bytes_accessed=2**20, transcendentals=0
        ),
    )(place_s, *updated)

    axes = ("macro", "pool")

    def hop(sent, mask):
        if mask == 0:
            return sent
        return lax.ppermute(sent, axes, [(s, s ^ mask) for s in range(devices)])

    two = jnp.concatenate([hop(sent, 2 * lanes) for sent in ready], axis=0)
    two, three, *singles = lax.optimization_barrier((two, three, *singles))
    lower = lax.axis_index(axes) < devices // 2
    pair = jnp.concatenate(
        [jnp.where(lower, two, three), jnp.where(lower, three, two)], axis=0
    ).reshape(2 * lanes, per_peer, deep)
    planes = [list(range(z * lanes, (z + 1) * lanes)) for z in range(PLANES)]
    pair = lax.all_to_all(
        pair, axes, split_axis=0, concat_axis=0, tiled=True,
        axis_index_groups=[planes[0] + planes[3], planes[1] + planes[2]],
    ).reshape(2 * group, deep)
    one = [hop(sent, lanes + i) for i, sent in enumerate(singles[:lanes])]
    own = [hop(sent, i) for i, sent in enumerate(singles[lanes:])]
    hbm = pl.BlockSpec(memory_space=pl.ANY)
    history_shape = jax.ShapeDtypeStruct((nodes, devices * per_peer), f32)
    staging = [pltpu.VMEM((4, nodes, LANES), f32), pltpu.SemaphoreType.DMA((4,))]
    new_history = pl.pallas_call(
        functools.partial(land_kernel, devices, per_peer),
        out_shape=history_shape,
        in_specs=[vmem] * (2 * lanes),
        out_specs=hbm,
        scratch_shapes=staging + [pltpu.VMEM((2, group, deep), f32)],
        compiler_params=params(),
    )(*own, *one)
    new_history = pl.pallas_call(
        functools.partial(last_kernel, devices),
        out_shape=history_shape,
        in_specs=[vmem, hbm],
        out_specs=hbm,
        scratch_shapes=staging,
        input_output_aliases={1: 0},
        compiler_params=params(),
    )(pair, new_history)
    stress_out = pl.pallas_call(
        back_kernel,
        out_shape=jax.ShapeDtypeStruct((voigt, columns), f32),
        in_specs=[vmem] * (1 + len(stress_s)),
        out_specs=vmem,
        compiler_params=params(),
    )(qp_s, *stress_s)
    return (new_history, stress_out)


def solution(mesh):
    return jax.shard_map(
        shards,
        mesh=mesh,
        in_specs=(
            P(None, ("macro", "pool")),
            P(None, ("macro", "pool")),
            P(None, ("macro", "pool")),
            P(("macro", "pool"), None),
            P(("macro", "pool"), None),
            P(),
            P(),
            P(),
            P(),
        ),
        out_specs=(P(None, ("macro", "pool")), P(None, ("macro", "pool"))),
        check_vma=False,
    )
```

time: 174 us -> 129 us (0.74)
  waiting for transfers between devices: 85.6 us -> 33.5 us
  starting transfers between devices: 31.2 us -> 34.7 us
  Pallas kernels: 42.4 us -> 45.8 us
    ppermute x6 -> x17, waiting for transfers between devices: 73.9 us -> 33.5 us  [hop(): return lax.ppermute(sent, axes, [(s, s ^ mask) for s in range(devices)])]
    ppermute x6 -> x17, starting transfers between devices: 11.7 us -> 27.7 us  [hop(): return lax.ppermute(sent, axes, [(s, s ^ mask) for s in range(devices)])]
    all_to_all x5 -> x1, starting transfers between devices: 19.5 us -> 6.93 us  [shards(): lax.all_to_all(pair, axes, split_axis=0, concat_axis=0, tiled=True, axis_...]
    all_to_all x5 -> x1, waiting for transfers between devices: 11.7 us -> 0.01 us  [shards(): lax.all_to_all(pair, axes, split_axis=0, concat_axis=0, tiled=True, axis_...]
    pallas_call x4 -> x3, Pallas kernels: 33.4 us -> 35.2 us  [shards(): pl.pallas_call(functools.partial(solve_kernel, 1.0 / math.sqrt(comps * no...]
    unnamed x20 -> x36, local copies, waits for them, and re-layouts: 9.94 us -> 10.8 us
  transfers between devices with their start and end apart: 11 -> 18, of which waited for: 9 -> 9; matrix products, arithmetic and copies ran while one was open for 2% -> 0% of each run, Pallas kernels for 1% -> 17%
where the time goes in v2:
time: 129 us; the launch traced here: 128 us
  Pallas kernels  45.8 us (36%)
  starting transfers between devices  34.7 us (27%)
  waiting for transfers between devices  33.5 us (26%)
  local copies, waits for them, and re-layouts  10.8 us (8%)
  other arithmetic  2.56 us (2%)
    pallas_call x3, Pallas kernels, shards(): pl.pallas_call(functools.partial(solve_kernel, 1.0 / math.sqrt(comps * no...  35.2 us
    ppermute x17, waiting for transfers between devices, hop(): return lax.ppermute(sent, axes, [(s, s ^ mask) for s in range(devices)])  33.5 us
    ppermute x17, starting transfers between devices, hop(): return lax.ppermute(sent, axes, [(s, s ^ mask) for s in range(devices)])  27.7 us
    unnamed x36, local copies, waits for them, and re-layouts  10.8 us
    all_to_all x1, starting transfers between devices, shards(): lax.all_to_all(pair, axes, split_axis=0, concat_axis=0, tiled=True, axis_...  6.93 us
    pallas_call x1, Pallas kernels, shards(): pl.pallas_call(functools.partial(prep_kernel, devices, per_peer), out_sha...  4.94 us
  transfers between devices with their start and end apart: 18, of which 9 were waited for; matrix products, arithmetic and copies ran while one was open for 0% of the time, Pallas kernels for 17%

profile of v2, /device:TPU:0, one launch (start us, length us, event | category | flops | bytes accessed | tf_op | source)
XLA Modules:
  0.0 128.3 jit_solution(17531618929002261001)
XLA Ops:
  5.0 4.9 %shard_map.104 = (bf16[736,768]{1,0:T(8,128)(2,1)S(1)}, bf16[736,768]{1,0:T(8,128)(2,1)S(1)}, f32[736,512]{1,0:T(8,128)S(1)}, f32[736,512]{1,0:T(8,128)S(1)}, f3...) custom-call(s32[1,512]{1,0:T(1,128)S(1)} %bitcast.4, ...), custom_call_target="tpu_custom_call" | custom-call | tf_op jit(solution)/shard_map/pallas_call | solution.py:317
  10.0 8.9 %shard_map.105 = (f32[736,128]{1,0:T(8,128)S(1)}, f32[8,128]{1,0:T(8,128)S(1)}, f32[128,768]{1,0:T(8,128)}) custom-call(bf16[736,768]{1,0:T(8,128)(2,1)S(1)} %get-tuple-element.54.khi, bf16[736,768]{1,0:T(8,128)(2,1)S(1)} %get-tuple-element.55.klo, f32[736,512]{1,0:T(8,128)S(1)} %get-tuple-element.56.hist, f32[736,512]{1,0:T(8,128)S(1)} %get-tuple-element.57.weight, ...), custom_call_target="tpu_custom_call" | custom-call | flops 434110464 | bytes 1048576 | tf_op jit(solution)/shard_map/pallas_call | solution.py:348
  18.9 9.0 %shard_map.106 = (f32[736,128]{1,0:T(8,128)S(1)}, f32[8,128]{1,0:T(8,128)S(1)}, f32[128,768]{1,0:T(8,128)}) custom-call(bf16[736,768]{1,0:T(8,128)(2,1)S(1)} %get-tuple-element.54.khi, bf16[736,768]{1,0:T(8,128)(2,1)S(1)} %get-tuple-element.55.klo, f32[736,512]{1,0:T(8,128)S(1)} %get-tuple-element.56.hist, f32[736,512]{1,0:T(8,128)S(1)} %get-tuple-element.57.weight, ...), custom_call_target="tpu_custom_call" | custom-call | flops 434110464 | bytes 1048576 | tf_op jit(solution)/shard_map/pallas_call | solution.py:348
  28.6 4.0 %collective-permute-start.1 = (f32[128,768]{1,0:T(8,128)}, f32[128,768]{1,0:T(8,128)}, u32[]{:S(2)}, u32[]{:S(2)}) collective-permute-start(f32[128,768]{1,0:T(8,128)} %get-tuple-element.64), channel_id=1, source_target_pairs={{0,16},{1,17},{2,18},{3,19},{4,20},{5,21},{6,22},{7,23},{8,24},{9,... | collective-permute-start | bytes 1179656 | tf_op jit(solution)/shard_map/ppermute | solution.py:387
  38.4 17.3 %shard_map.107 = (f32[736,256]{1,0:T(8,128)S(1)}, f32[8,256]{1,0:T(8,128)S(1)}) custom-call(bf16[736,768]{1,0:T(8,128)(2,1)S(1)} %copy-done.1, bf16[736,768]{1,0:T(8,128)(2,1)S(1)} %copy-done.3, f32[736,512]{1,0:T(8,128)S(1)} %get-tuple-element.56.hist, f32[736,512]{1,0:T(8,128)S(1)} %get-tuple-element.57.weight, f32[8,512]{1,0:T(8,128)S(1)} %get-tuple-element.58.strain, ...), custom_call_target="tpu_custom_call" | custom-call | flops 868220928 | bytes 1048576 | tf_op jit(solution)/shard_map/pallas_call | solution.py:348
  55.7 2.1 %shard_map.108 = (f32[256,768]{1,0:T(8,128)S(1)}, f32[32,768]{1,0:T(8,128)S(1)}, f32[32,768]{1,0:T(8,128)S(1)}, f32[32,768]{1,0:T(8,128)S(1)}, f32[32,768]{1,0:T...) custom-call(s32[8,512]{1,0:T(8,128)S(1)} %get-tuple-element.61.place, ...), custom_call_target="tpu_custom_call" | custom-call | flops 1048576 | bytes 1048576 | tf_op jit(solution)/shard_map/pallas_call | solution.py:371
  57.8 2.0 %collective-permute-done.1 = f32[128,768]{1,0:T(8,128)} collective-permute-done((f32[128,768]{1,0:T(8,128)}, f32[128,768]{1,0:T(8,128)}, u32[]{:S(2)}, u32[]{:S(2)}) %collective-permute-start.1) | collective-permute-done | bytes 393248 | tf_op jit(solution)/shard_map/ppermute | solution.py:387
  59.8 7.6 %collective-permute-done = f32[128,768]{1,0:T(8,128)} collective-permute-done((f32[128,768]{1,0:T(8,128)}, f32[128,768]{1,0:T(8,128)}, u32[]{:S(2)}, u32[]{:S(2)}) %collective-permute-start) | collective-permute-done | bytes 393248 | tf_op jit(solution)/shard_map/ppermute | solution.py:387
  68.7 1.3 pad_maximum_fusion
  70.0 6.9 %all-to-all-start = ((f32[16,32,768]{2,1,0:T(8,128)}), f32[16,32,768]{2,1,0:T(8,128)S(1)}, u32[]{:S(2)}, u32[]{:S(2)}) async-start(f32[16,32,768]{2,1,0:T(8,128)} %bitcast.5), calls=%async_computation | async-start | bytes 3145728 | tf_op jit(solution)/shard_map/all_to_all | solution.py:396
  77.0 3.1 %collective-permute-start.11 = (f32[32,768]{1,0:T(8,128)S(1)}, f32[32,768]{1,0:T(8,128)S(1)}, u32[]{:S(2)}, u32[]{:S(2)}) collective-permute-start(f32[32,768]{1,0:T(8,128)S(1)} %get-tuple-element.96), channel_id=1, source_target_pairs={{0,10},{1,11},{2,8},{3,9},{4,14},{5,15},{6,12},{7,13},{8,2},{9,3},... | collective-permute-start | bytes 294920 | tf_op jit(solution)/shard_map/ppermute | solution.py:387
  80.1 2.6 %collective-permute-start.13 = (f32[32,768]{1,0:T(8,128)S(1)}, f32[32,768]{1,0:T(8,128)S(1)}, u32[]{:S(2)}, u32[]{:S(2)}) collective-permute-start(f32[32,768]{1,0:T(8,128)S(1)} %get-tuple-element.98), channel_id=1, source_target_pairs={{0,12},{1,13},{2,14},{3,15},{4,8},{5,9},{6,10},{7,11},{8,4},{9,5},... | collective-permute-start | bytes 294920 | tf_op jit(solution)/shard_map/ppermute | solution.py:387
  82.8 14.6 %collective-permute-done.10.refs_9_ = f32[32,768]{1,0:T(8,128)S(1)} collective-permute-done((f32[32,768]{1,0:T(8,128)S(1)}, f32[32,768]{1,0:T(8,128)S(1)}, u32[]{:S(2)}, u32[]{:S(2)}) %collective-permute-start.10) | collective-permute-done | bytes 98336 | tf_op jit(solution)/shard_map/ppermute | solution.py:387
  97.4 4.3 %collective-permute-start.15 = (f32[32,768]{1,0:T(8,128)S(1)}, f32[32,768]{1,0:T(8,128)S(1)}, u32[]{:S(2)}, u32[]{:S(2)}) collective-permute-start(f32[32,768]{1,0:T(8,128)S(1)} %get-tuple-element.100), channel_id=1, source_target_pairs={{0,14},{1,15},{2,12},{3,13},{4,10},{5,11},{6,8},{7,9},{8,6},{9,7},... | collective-permute-start | bytes 294920 | tf_op jit(solution)/shard_map/ppermute | solution.py:387
  102.8 2.3 %collective-permute-start.16 = (f32[32,768]{1,0:T(8,128)S(1)}, f32[32,768]{1,0:T(8,128)S(1)}, u32[]{:S(2)}, u32[]{:S(2)}) collective-permute-start(f32[32,768]{1,0:T(8,128)S(1)} %get-tuple-element.101), channel_id=1, source_target_pairs={{0,15},{1,14},{2,13},{3,12},{4,11},{5,10},{6,9},{7,8},{8,7},{9,6},... | collective-permute-start | bytes 294920 | tf_op jit(solution)/shard_map/ppermute | solution.py:387
  105.1 2.5 %collective-permute-start.2 = (f32[32,768]{1,0:T(8,128)S(1)}, f32[32,768]{1,0:T(8,128)S(1)}, u32[]{:S(2)}, u32[]{:S(2)}) collective-permute-start(f32[32,768]{1,0:T(8,128)S(1)} %get-tuple-element.87), channel_id=1, source_target_pairs={{0,1},{1,0},{2,3},{3,2},{4,5},{5,4},{6,7},{7,6},{8,9},{9,8},{10,11... | collective-permute-start | bytes 294920 | tf_op jit(solution)/shard_map/ppermute | solution.py:387
  109.9 3.6 %collective-permute-done.15.refs_14_ = f32[32,768]{1,0:T(8,128)S(1)} collective-permute-done((f32[32,768]{1,0:T(8,128)S(1)}, f32[32,768]{1,0:T(8,128)S(1)}, u32[]{:S(2)}, u32[]{:S(2)}) %collective-permute-start.15) | collective-permute-done | bytes 98336 | tf_op jit(solution)/shard_map/ppermute | solution.py:387
  114.5 1.5 %collective-permute-done.16.refs_15_ = f32[32,768]{1,0:T(8,128)S(1)} collective-permute-done((f32[32,768]{1,0:T(8,128)S(1)}, f32[32,768]{1,0:T(8,128)S(1)}, u32[]{:S(2)}, u32[]{:S(2)}) %collective-permute-start.16) | collective-permute-done | bytes 98336 | tf_op jit(solution)/shard_map/ppermute | solution.py:387
  115.9 1.3 collective-permute-start.7
  117.2 1.4 %collective-permute-start.8 = (f32[32,768]{1,0:T(8,128)S(1)}, f32[32,768]{1,0:T(8,128)S(1)}, u32[]{:S(2)}, u32[]{:S(2)}) collective-permute-start(f32[32,768]{1,0:T(8,128)S(1)} %get-tuple-element.93), channel_id=1, source_target_pairs={{0,7},{1,6},{2,5},{3,4},{4,3},{5,2},{6,1},{7,0},{8,15},{9,14},{10,... | collective-permute-start | bytes 294920 | tf_op jit(solution)/shard_map/ppermute | solution.py:387
  118.6 3.3 %collective-permute-start.9 = (f32[32,768]{1,0:T(8,128)S(1)}, f32[32,768]{1,0:T(8,128)S(1)}, u32[]{:S(2)}, u32[]{:S(2)}) collective-permute-start(f32[32,768]{1,0:T(8,128)S(1)} %get-tuple-element.94), channel_id=1, source_target_pairs={{0,8},{1,9},{2,10},{3,11},{4,12},{5,13},{6,14},{7,15},{8,0},{9,1},... | collective-permute-start | bytes 294920 | tf_op jit(solution)/shard_map/ppermute | solution.py:387
  122.8 2.3 %collective-permute-done.6.refs_5_ = f32[32,768]{1,0:T(8,128)S(1)} collective-permute-done((f32[32,768]{1,0:T(8,128)S(1)}, f32[32,768]{1,0:T(8,128)S(1)}, u32[]{:S(2)}, u32[]{:S(2)}) %collective-permute-start.6) | collective-permute-done | bytes 98336 | tf_op jit(solution)/shard_map/ppermute | solution.py:387
  125.4 1.4 %shard_map.109.history = f32[729,1024]{1,0:T(8,128)} custom-call(f32[32,768]{1,0:T(8,128)S(1)} %get-tuple-element.86.refs_0_, f32[32,768]{1,0:T(8,128)S(1)} %collective-permute-done.2.refs_1_, f32[32,768]{1,0:T(8,128)S(1)} %collective-permute-done.3.refs_2_, f32[32,768]{1,0:T(8,128)S(1)} %collective-permute-done.4.refs_3_, ...), custom_call_target="tpu_custom_call" | custom-call | tf_op jit(solution)/shard_map/pallas_call | solution.py:405
  126.8 1.3 %shard_map.110 = f32[729,1024]{1,0:T(8,128)} custom-call(f32[512,768]{1,0:T(8,128)S(1)} %bitcast.3, f32[729,1024]{1,0:T(8,128)} %shard_map.109.history), custom_call_target="tpu_custom_call", output_to_operand_aliasing={{}: (1, {})} | custom-call | tf_op jit(solution)/shard_map/pallas_call | solution.py:413
  (59 shorter events, 17.7 us)
Async XLA Ops:
  10.0 8.9 %copy-start = (bf16[736,768]{1,0:T(8,128)(2,1)}, bf16[736,768]{1,0:T(8,128)(2,1)S(1)}, u32[]{:S(2)}) copy-start(bf16[736,768]{1,0:T(8,128)(2,1)S(1)} %get-tuple-element.54.khi) | copy-start | bytes 3391492
  10.0 8.9 %copy-start.2 = (bf16[736,768]{1,0:T(8,128)(2,1)}, bf16[736,768]{1,0:T(8,128)(2,1)S(1)}, u32[]{:S(2)}) copy-start(bf16[736,768]{1,0:T(8,128)(2,1)S(1)} %get-tuple-element.55.klo) | copy-start | bytes 3391492
  10.0 8.9 %copy-start.4 = (f32[3,736,128]{2,1,0:T(8,128)}, f32[3,736,128]{2,1,0:T(8,128)S(1)}, u32[]{:S(2)}) copy-start(f32[3,736,128]{2,1,0:T(8,128)S(1)} %get-tuple-element.60.pdir) | copy-start | bytes 3391492
  10.0 8.9 %copy-start.6 = (f32[3,32,736]{2,1,0:T(8,128)}, f32[3,32,736]{2,1,0:T(8,128)S(1)}, u32[]{:S(2)}) copy-start(f32[3,32,736]{2,1,0:T(8,128)S(1)} %get-tuple-element.59.cstack) | copy-start | bytes 847876
  28.6 31.2 %collective-permute-start.1 = (f32[128,768]{1,0:T(8,128)}, f32[128,768]{1,0:T(8,128)}, u32[]{:S(2)}, u32[]{:S(2)}) collective-permute-start(f32[128,768]{1,0:T(8,128)} %get-tuple-element.64), channel_id=1, source_target_pairs={{0,16},{1,17},{2,18},{3,19},{4,20},{5,21},{6,22},{7,23},{8,24},{9,... | collective-permute-start | bytes 1179656 | tf_op jit(solution)/shard_map/ppermute | solution.py:387
  32.7 34.7 %collective-permute-start = (f32[128,768]{1,0:T(8,128)}, f32[128,768]{1,0:T(8,128)}, u32[]{:S(2)}, u32[]{:S(2)}) collective-permute-start(f32[128,768]{1,0:T(8,128)} %get-tuple-element.62), channel_id=1, source_target_pairs={{0,16},{1,17},{2,18},{3,19},{4,20},{5,21},{6,22},{7,23},{8,24},{9,... | collective-permute-start | bytes 1179656 | tf_op jit(solution)/shard_map/ppermute | solution.py:387
  57.8 10.9 %copy-start.16 = (f32[32,768]{1,0:T(8,128)}, f32[32,768]{1,0:T(8,128)S(1)}, u32[]{:S(2)}) copy-start(f32[32,768]{1,0:T(8,128)S(1)} %get-tuple-element.95) | copy-start | bytes 294916
  70.0 6.9 %copy-start.17 = (f32[32,768]{1,0:T(8,128)S(1)}, f32[32,768]{1,0:T(8,128)}, u32[]{:S(2)}) copy-start(f32[32,768]{1,0:T(8,128)} %copy-done.16) | copy-start | bytes 294916
  70.0 56.8 %all-to-all-start = ((f32[16,32,768]{2,1,0:T(8,128)}), f32[16,32,768]{2,1,0:T(8,128)S(1)}, u32[]{:S(2)}, u32[]{:S(2)}) async-start(f32[16,32,768]{2,1,0:T(8,128)} %bitcast.5), calls=%async_computation | async-start | bytes 3145728 | tf_op jit(solution)/shard_map/all_to_all | solution.py:396
  76.9 20.5 %collective-permute-start.10 = (f32[32,768]{1,0:T(8,128)S(1)}, f32[32,768]{1,0:T(8,128)S(1)}, u32[]{:S(2)}, u32[]{:S(2)}) collective-permute-start(f32[32,768]{1,0:T(8,128)S(1)} %copy-done.17), channel_id=1, source_target_pairs={{0,9},{1,8},{2,11},{3,10},{4,13},{5,12},{6,15},{7,14},{8,1},{9,0},... | collective-permute-start | bytes 294920 | tf_op jit(solution)/shard_map/ppermute | solution.py:387
  77.0 25.8 %collective-permute-start.11 = (f32[32,768]{1,0:T(8,128)S(1)}, f32[32,768]{1,0:T(8,128)S(1)}, u32[]{:S(2)}, u32[]{:S(2)}) collective-permute-start(f32[32,768]{1,0:T(8,128)S(1)} %get-tuple-element.96), channel_id=1, source_target_pairs={{0,10},{1,11},{2,8},{3,9},{4,14},{5,15},{6,12},{7,13},{8,2},{9,3},... | collective-permute-start | bytes 294920 | tf_op jit(solution)/shard_map/ppermute | solution.py:387
  80.1 24.9 %collective-permute-start.12 = (f32[32,768]{1,0:T(8,128)S(1)}, f32[32,768]{1,0:T(8,128)S(1)}, u32[]{:S(2)}, u32[]{:S(2)}) collective-permute-start(f32[32,768]{1,0:T(8,128)S(1)} %get-tuple-element.97), channel_id=1, source_target_pairs={{0,11},{1,10},{2,9},{3,8},{4,15},{5,14},{6,13},{7,12},{8,3},{9,2},... | collective-permute-start | bytes 294920 | tf_op jit(solution)/shard_map/ppermute | solution.py:387
  80.1 27.5 %collective-permute-start.13 = (f32[32,768]{1,0:T(8,128)S(1)}, f32[32,768]{1,0:T(8,128)S(1)}, u32[]{:S(2)}, u32[]{:S(2)}) collective-permute-start(f32[32,768]{1,0:T(8,128)S(1)} %get-tuple-element.98), channel_id=1, source_target_pairs={{0,12},{1,13},{2,14},{3,15},{4,8},{5,9},{6,10},{7,11},{8,4},{9,5},... | collective-permute-start | bytes 294920 | tf_op jit(solution)/shard_map/ppermute | solution.py:387
  82.7 26.3 %collective-permute-start.14 = (f32[32,768]{1,0:T(8,128)S(1)}, f32[32,768]{1,0:T(8,128)S(1)}, u32[]{:S(2)}, u32[]{:S(2)}) collective-permute-start(f32[32,768]{1,0:T(8,128)S(1)} %get-tuple-element.99), channel_id=1, source_target_pairs={{0,13},{1,12},{2,15},{3,14},{4,9},{5,8},{6,11},{7,10},{8,5},{9,4},... | collective-permute-start | bytes 294920 | tf_op jit(solution)/shard_map/ppermute | solution.py:387
  97.4 16.1 %collective-permute-start.15 = (f32[32,768]{1,0:T(8,128)S(1)}, f32[32,768]{1,0:T(8,128)S(1)}, u32[]{:S(2)}, u32[]{:S(2)}) collective-permute-start(f32[32,768]{1,0:T(8,128)S(1)} %get-tuple-element.100), channel_id=1, source_target_pairs={{0,14},{1,15},{2,12},{3,13},{4,10},{5,11},{6,8},{7,9},{8,6},{9,7},... | collective-permute-start | bytes 294920 | tf_op jit(solution)/shard_map/ppermute | solution.py:387
  102.8 13.2 %collective-permute-start.16 = (f32[32,768]{1,0:T(8,128)S(1)}, f32[32,768]{1,0:T(8,128)S(1)}, u32[]{:S(2)}, u32[]{:S(2)}) collective-permute-start(f32[32,768]{1,0:T(8,128)S(1)} %get-tuple-element.101), channel_id=1, source_target_pairs={{0,15},{1,14},{2,13},{3,12},{4,11},{5,10},{6,9},{7,8},{8,7},{9,6},... | collective-permute-start | bytes 294920 | tf_op jit(solution)/shard_map/ppermute | solution.py:387
  105.1 10.9 %collective-permute-start.2 = (f32[32,768]{1,0:T(8,128)S(1)}, f32[32,768]{1,0:T(8,128)S(1)}, u32[]{:S(2)}, u32[]{:S(2)}) collective-permute-start(f32[32,768]{1,0:T(8,128)S(1)} %get-tuple-element.87), channel_id=1, source_target_pairs={{0,1},{1,0},{2,3},{3,2},{4,5},{5,4},{6,7},{7,6},{8,9},{9,8},{10,11... | collective-permute-start | bytes 294920 | tf_op jit(solution)/shard_map/ppermute | solution.py:387
  107.6 9.6 %collective-permute-start.3 = (f32[32,768]{1,0:T(8,128)S(1)}, f32[32,768]{1,0:T(8,128)S(1)}, u32[]{:S(2)}, u32[]{:S(2)}) collective-permute-start(f32[32,768]{1,0:T(8,128)S(1)} %get-tuple-element.88), channel_id=1, source_target_pairs={{0,2},{1,3},{2,0},{3,1},{4,6},{5,7},{6,4},{7,5},{8,10},{9,11},{10,... | collective-permute-start | bytes 294920 | tf_op jit(solution)/shard_map/ppermute | solution.py:387
  109.1 9.6 %collective-permute-start.4 = (f32[32,768]{1,0:T(8,128)S(1)}, f32[32,768]{1,0:T(8,128)S(1)}, u32[]{:S(2)}, u32[]{:S(2)}) collective-permute-start(f32[32,768]{1,0:T(8,128)S(1)} %get-tuple-element.89), channel_id=1, source_target_pairs={{0,3},{1,2},{2,1},{3,0},{4,7},{5,6},{6,5},{7,4},{8,11},{9,10},{10,... | collective-permute-start | bytes 294920 | tf_op jit(solution)/shard_map/ppermute | solution.py:387
  113.5 9.3 %collective-permute-start.5 = (f32[32,768]{1,0:T(8,128)S(1)}, f32[32,768]{1,0:T(8,128)S(1)}, u32[]{:S(2)}, u32[]{:S(2)}) collective-permute-start(f32[32,768]{1,0:T(8,128)S(1)} %get-tuple-element.90), channel_id=1, source_target_pairs={{0,4},{1,5},{2,6},{3,7},{4,0},{5,1},{6,2},{7,3},{8,12},{9,13},{10,... | collective-permute-start | bytes 294920 | tf_op jit(solution)/shard_map/ppermute | solution.py:387
  115.9 9.2 %collective-permute-start.6 = (f32[32,768]{1,0:T(8,128)S(1)}, f32[32,768]{1,0:T(8,128)S(1)}, u32[]{:S(2)}, u32[]{:S(2)}) collective-permute-start(f32[32,768]{1,0:T(8,128)S(1)} %get-tuple-element.91), channel_id=1, source_target_pairs={{0,5},{1,4},{2,7},{3,6},{4,1},{5,0},{6,3},{7,2},{8,13},{9,12},{10,... | collective-permute-start | bytes 294920 | tf_op jit(solution)/shard_map/ppermute | solution.py:387
  115.9 9.2 %collective-permute-start.7 = (f32[32,768]{1,0:T(8,128)S(1)}, f32[32,768]{1,0:T(8,128)S(1)}, u32[]{:S(2)}, u32[]{:S(2)}) collective-permute-start(f32[32,768]{1,0:T(8,128)S(1)} %get-tuple-element.92), channel_id=1, source_target_pairs={{0,6},{1,7},{2,4},{3,5},{4,2},{5,3},{6,0},{7,1},{8,14},{9,15},{10,... | collective-permute-start | bytes 294920 | tf_op jit(solution)/shard_map/ppermute | solution.py:387
  117.2 7.9 %collective-permute-start.8 = (f32[32,768]{1,0:T(8,128)S(1)}, f32[32,768]{1,0:T(8,128)S(1)}, u32[]{:S(2)}, u32[]{:S(2)}) collective-permute-start(f32[32,768]{1,0:T(8,128)S(1)} %get-tuple-element.93), channel_id=1, source_target_pairs={{0,7},{1,6},{2,5},{3,4},{4,3},{5,2},{6,1},{7,0},{8,15},{9,14},{10,... | collective-permute-start | bytes 294920 | tf_op jit(solution)/shard_map/ppermute | solution.py:387
  118.6 6.7 %collective-permute-start.9 = (f32[32,768]{1,0:T(8,128)S(1)}, f32[32,768]{1,0:T(8,128)S(1)}, u32[]{:S(2)}, u32[]{:S(2)}) collective-permute-start(f32[32,768]{1,0:T(8,128)S(1)} %get-tuple-element.94), channel_id=1, source_target_pairs={{0,8},{1,9},{2,10},{3,11},{4,12},{5,13},{6,14},{7,15},{8,0},{9,1},... | collective-permute-start | bytes 294920 | tf_op jit(solution)/shard_map/ppermute | solution.py:387
  (12 other events, 10.8 us)
